TPU v7x, 32 devices: a whole 2x2x4 slice. The times are simulated.
32 devices in a mesh: seq: 8 (over z, y), tp: 4 (over x, core).
Axes of the slice: x: 2, y: 2, z: 4, core: 2. Of those that a mesh axis runs over, the one named last changes fastest.
Arguments:
- tokens: bfloat16 [128, 1536], replicated, may hold values from -6 to 6
- attn_gain: float32 [1536], replicated, may hold values from 0.25 to 1.75
- qkv_weight: bfloat16 [1536, 2560], P(None, 'tp'), may hold values from -0.15625 to 0.15625
- out_weight: bfloat16 [1536, 1536], P(None, 'tp'), may hold values from -0.15625 to 0.15625
- moe_gain: float32 [1536], P('tp'), may hold values from 0.25 to 1.75
- router_weight: bfloat16 [1536, 40], P('tp'), may hold values from -0.3125 to 0.3125
- expert_gate: bfloat16 [40, 1536, 512], P(None, 'tp', 'seq'), may hold values from -0.15625 to 0.15625
- expert_up: bfloat16 [40, 1536, 512], P(None, 'tp', 'seq'), may hold values from -0.15625 to 0.15625
- expert_down: bfloat16 [40, 512, 1536], P(None, 'seq', 'tp'), may hold values from -0.375 to 0.375
- cache_keys: bfloat16 [32, 256, 512], P(None, 'seq', 'tp'), may hold values from -240 to 240, as said below
- cache_values: bfloat16 [32, 256, 512], P(None, 'seq', 'tp'), may hold values from -8 to 8
- lengths: int32 [32], replicated, may hold values from 1 to 32768, as said below
- routes: int32 [128, 8], replicated, may hold values from 0 to 39, all different within a row
Outputs:
- layer_out: bfloat16 [128, 1536], P(None, 'tp')
Inputs may be any that keep to these rules, and one draw needn't show every extreme that they name: `lengths`: one request has exactly 32768 cached positions. `cache_keys`: cached keys are already rotated.
All inputs are finite; a program needn't handle non-finite values.
Results may differ from a plain program's by a relative error of at most 0.014.
Values may be sent and summed in bfloat16 or wider, within the bound.
A program may use at most 128 MiB of HBM per device.

v0:
```python
import jax
import jax.numpy as jnp
from jax import lax
from jax.sharding import PartitionSpec as P

D = 1536
HEAD = 64
EXPERTS = 40
SINK = 4
NEW = 4
GROUP = 3


EPSILON = 1e-06
ROPE_BASE = 10000.0
FLOOR_SCORE = -1e30


def joined(shard, axis, combine):
    everything = jax.tree.map(lambda part: lax.all_gather(part, axis), shard)
    initial = jax.tree.map(lambda part: part[0], everything)

    def lap(k, so_far):
        return combine(so_far, jax.tree.map(lambda part: part[k], everything))

    return lax.fori_loop(1, lax.axis_size(axis), lap, initial)


def rms_scale(values, gain):
    return values * lax.rsqrt(jnp.mean(values * values, axis=-1, keepdims=True) + EPSILON) * gain


def rotate(values, places):
    half_dim = values.shape[-1] // 2
    freqs = jnp.exp(-jnp.log(ROPE_BASE) * jnp.arange(half_dim, dtype=jnp.float32) / half_dim)
    angles = places.reshape((-1,) + (1,) * (values.ndim - 1)) * freqs
    cosine = jnp.cos(angles)
    sine = jnp.sin(angles)
    first = values[..., :half_dim]
    second = values[..., half_dim:]
    return jnp.concatenate(
        [first * cosine - second * sine, first * sine + second * cosine], axis=-1
    )


def visible(slots, lengths, window):
    lens = lengths[:, None]
    slot_row = slots[None, :]
    live = slot_row < lens
    older = lens - 1 - jnp.mod(lens - 1 - slot_row, window)
    placed = jnp.where(slot_row < SINK, slot_row, older)
    offsets = jnp.arange(NEW, dtype=jnp.int32)
    inside = (slot_row[:, None, :] < SINK) | (
        placed[:, None, :] >= lens[:, :, None] + offsets[None, :, None] - window
    )
    return live[:, None, :] & inside


def combine_parts(earlier, later):
    top_a, mass_a, weighted_a = earlier
    top_b, mass_b, weighted_b = later
    top_both = jnp.maximum(top_a, top_b)
    factor_a = jnp.exp(top_a - top_both)
    factor_b = jnp.exp(top_b - top_both)
    return (
        top_both,
        mass_a * factor_a + mass_b * factor_b,
        weighted_a * factor_a[..., None] + weighted_b * factor_b[..., None],
    )


def on_device(
    tokens,
    attn_gain,
    qkv_weight,
    out_weight,
    moe_gain,
    router_weight,
    expert_gate,
    expert_up,
    expert_down,
    cache_keys,
    cache_values,
    lengths,
    routes,
):
    seq_count = lax.axis_size("seq")
    seq_index = lax.axis_index("seq")
    tp_index = lax.axis_index("tp")
    token_count = tokens.shape[0]
    requests = cache_keys.shape[0]
    slot_count = cache_keys.shape[1]
    window = slot_count * seq_count - SINK
    local_kv = cache_keys.shape[2] // HEAD
    token_full = tokens.astype(jnp.float32)
    normed = rms_scale(token_full, attn_gain).astype(jnp.bfloat16)
    projected = jnp.dot(normed, qkv_weight, preferred_element_type=jnp.float32)
    projected = projected.reshape(token_count, local_kv, GROUP + 2, HEAD)
    places = (
        (lengths[:, None] + jnp.arange(NEW, dtype=jnp.int32)[None, :])
        .reshape(token_count)
        .astype(jnp.float32)
    )
    queries = rotate(projected[:, :, :GROUP], places).astype(jnp.bfloat16)
    new_keys = rotate(projected[:, :, GROUP], places).astype(jnp.bfloat16)
    new_values = projected[:, :, GROUP + 1].astype(jnp.bfloat16)
    query_b = queries.reshape(requests, NEW, local_kv, GROUP, HEAD)
    key_new = new_keys.reshape(requests, NEW, local_kv, HEAD)
    value_new = new_values.reshape(requests, NEW, local_kv, HEAD)
    slots = seq_index * slot_count + jnp.arange(slot_count, dtype=jnp.int32)
    seen = visible(slots, lengths, window)[:, :, None, None, :]
    factor = 1.0 / HEAD**0.5
    key_old = cache_keys.reshape(requests, slot_count, local_kv, HEAD)
    value_old = cache_values.reshape(requests, slot_count, local_kv, HEAD)
    old_scores = (
        jnp.einsum("rtgqd,rsgd->rtgqs", query_b, key_old, preferred_element_type=jnp.float32)
        * factor
    )
    new_scores = (
        jnp.einsum("rtgqd,rugd->rtgqu", query_b, key_new, preferred_element_type=jnp.float32)
        * factor
    )
    causal = jnp.arange(NEW)[:, None] >= jnp.arange(NEW)[None, :]
    own_mask = causal[None, :, None, None, :] & (seq_index == 0)
    old_masked = jnp.where(seen, old_scores, FLOOR_SCORE)
    new_masked = jnp.where(own_mask, new_scores, FLOOR_SCORE)
    top_score = jnp.maximum(jnp.max(old_masked, axis=-1), jnp.max(new_masked, axis=-1))
    old_weights = jnp.where(seen, jnp.exp(old_masked - top_score[..., None]), 0.0)
    new_weights = jnp.where(own_mask, jnp.exp(new_masked - top_score[..., None]), 0.0)
    mass = jnp.sum(old_weights, axis=-1) + jnp.sum(new_weights, axis=-1)
    weighted = jnp.einsum(
        "rtgqs,rsgd->rtgqd", old_weights, value_old.astype(jnp.float32)
    ) + jnp.einsum("rtgqu,rugd->rtgqd", new_weights, value_new.astype(jnp.float32))
    top_score, mass, weighted = joined((top_score, mass, weighted), "seq", combine_parts)
    attended = (weighted / mass[..., None]).reshape(token_count, -1).astype(jnp.bfloat16)
    feature_part = out_weight.shape[1]
    attn_out = jnp.dot(
        lax.all_gather(attended, "tp", axis=1, tiled=True),
        out_weight,
        preferred_element_type=jnp.float32,
    )
    residual = (
        lax.dynamic_slice_in_dim(token_full, tp_index * feature_part, feature_part, 1) + attn_out
    )
    gained = residual * moe_gain
    squares_local = jnp.sum(residual * residual, axis=-1)
    router_f = router_weight.astype(jnp.float32)
    squares_total = lax.psum(squares_local, "tp")
    scale = lax.rsqrt(squares_total / D + EPSILON)
    logits = lax.psum(
        jnp.dot(gained * scale[:, None], router_f, precision=lax.Precision.HIGHEST), "tp"
    )
    moe_in = (gained * scale[:, None]).astype(jnp.bfloat16)
    chosen = jnp.take_along_axis(logits, routes, axis=1)
    gate_prob = jax.nn.softmax(chosen, axis=-1)
    gate_part = jnp.einsum("td,edf->tef", moe_in, expert_gate, preferred_element_type=jnp.float32)
    up_part = jnp.einsum("td,edf->tef", moe_in, expert_up, preferred_element_type=jnp.float32)
    gate_pick = jnp.take_along_axis(gate_part, routes[:, :, None], axis=1)
    up_pick = jnp.take_along_axis(up_part, routes[:, :, None], axis=1)
    gate_sum, up_sum = (
        lax.psum(gate_pick.astype(jnp.bfloat16), "tp").astype(jnp.float32),
        lax.psum(up_pick.astype(jnp.bfloat16), "tp").astype(jnp.float32),
    )
    activated = (jax.nn.silu(gate_sum) * up_sum).astype(jnp.bfloat16)
    scaled = (gate_prob[:, :, None] * activated.astype(jnp.float32)).astype(jnp.bfloat16)
    onehot = (routes[:, :, None] == jnp.arange(EXPERTS, dtype=jnp.int32)[None, None, :]).astype(
        jnp.bfloat16
    )
    spread = jnp.einsum("tke,tkf->tef", onehot, scaled, preferred_element_type=jnp.float32).astype(
        jnp.bfloat16
    )
    moe_part = jnp.einsum("tef,efd->td", spread, expert_down, preferred_element_type=jnp.float32)
    moe_out = lax.psum(moe_part, "seq")
    return (residual + moe_out).astype(jnp.bfloat16)


def solution(mesh):
    in_specs = (
        P(),
        P(),
        P(None, "tp"),
        P(None, "tp"),
        P("tp"),
        P("tp", None),
        P(None, "tp", "seq"),
        P(None, "tp", "seq"),
        P(None, "seq", "tp"),
        P(None, "seq", "tp"),
        P(None, "seq", "tp"),
        P(),
        P(),
    )
    out_specs = P(None, "tp")
    return jax.shard_map(
        on_device, mesh=mesh, in_specs=in_specs, out_specs=out_specs, check_vma=False
    )
```

profile of v0, /device:TPU:0, one launch (start us, length us, event | category | flops | bytes accessed | tf_op | source)
XLA Modules:
  0.0 302.5 jit_solution(8245899872915523931)
XLA Ops:
  9.3 2.6 fusion.23
  14.4 1.2 reshape.397
  16.8 1.5 fusion.66
  18.8 1.2 fusion.6
  22.2 35.2 %all-gather.1 = f32[256,4,2,3]{1,2,3,0:T(2,128)S(1)} all-gather(f32[32,4,2,3]{1,2,3,0:T(2,128)S(1)} %copy.118), channel_id=3, replica_groups=mesh['seq'=8,'tp'=4] {'seq'}, dimensions={0}, use_global_device_ids=true | all-gather | bytes 27648 | tf_op jit(solution)/shard_map/all_gather | solution.py:20
  58.1 34.3 %all-gather = f32[256,4,2,3]{1,2,3,0:T(2,128)S(1)} all-gather(f32[32,4,2,3]{1,2,3,0:T(2,128)S(1)} %copy.117), channel_id=2, replica_groups=mesh['seq'=8,'tp'=4] {'seq'}, dimensions={0}, use_global_device_ids=true | all-gather | bytes 27648 | tf_op jit(solution)/shard_map/all_gather | solution.py:20
  94.4 6.2 %all-gather.5.cloned.1.call-done = f32[256,4,2,3,64]{4,1,3,2,0:T(4,128)} async-done(((f32[32,4,2,3,64]{4,1,3,2,0:T(4,128)}), f32[256,4,2,3,64]{4,1,3,2,0:T(4,128)}) %all-gather.5.cloned.1.call-update) | async-done | bytes 1572880 | tf_op jit(solution)/shard_map/all_gather | solution.py:20
  101.9 17.1 %while.19 = (s32[]{:T(128)}, f32[32,4,2,3]{0,2,3,1:T(2,128)S(1)}, f32[32,4,2,3]{0,2,3,1:T(2,128)S(1)}, f32[32,4,2,3,64]{4,3,2,1,0:T(4,128)S(1)}, f32[8,32,4,2,3]...) while((s32[]{:T(128)}, f32[32,4,2,3]{0,2,3,1:T(2,128)S(1)}, ...), condition=%wide.region_6.7_spmd, body=%wide.region_5.6_spmd.sunk | while | flops 152069 | bytes 1026199 | solution.py:26
  119.8 6.4 %all_gather.21 = bf16[128,1536]{1,0:T(8,128)(2,1)S(1)} all-gather(bf16[128,384]{1,0:T(8,128)(2,1)S(1)} %convert_element_type.75), channel_id=1, replica_groups=mesh['seq'=8,'tp'=4] {'tp'}, dimensions={1}, use_global_device_ids=true | all-gather | bytes 491520 | tf_op jit(solution)/shard_map/all_gather | solution.py:138
  126.2 1.8 multiply_reduce_fusion.1
  128.0 6.8 %psum.35 = f32[128]{0:T(128)S(1)} all-reduce(f32[128]{0:T(128)S(1)} %get-tuple-element.249), channel_id=1, replica_groups=mesh['seq'=8,'tp'=4] {'tp'}, use_global_device_ids=true, to_apply=%region_8.9 | all-reduce | flops 128 | bytes 1024 | tf_op jit(solution)/shard_map/psum | solution.py:148
  135.1 10.7 %psum.36 = f32[128,40]{0,1:T(8,128)S(1)} all-reduce(f32[128,40]{0,1:T(8,128)S(1)} %fusion.39), channel_id=1, replica_groups=mesh['seq'=8,'tp'=4] {'tp'}, use_global_device_ids=true, to_apply=%region_9.10 | all-reduce | flops 5120 | bytes 40960 | tf_op jit(solution)/shard_map/psum | solution.py:150
  145.8 7.0 %gather_fusion = f32[1024]{0:T(1024)S(1)} fusion(f32[128,40]{0,1:T(8,128)S(1)} %psum.36, s32[1024]{0:T(1024)S(1)} %reshape.411), kind=kCustom, calls=%fused_computation.2 | custom fusion | bytes 16384 | tf_op jit(solution)/shard_map/jit(take_along_axis)/gather | solution.py:154
  153.0 1.8 fusion.60
  154.9 2.5 copy.141
  157.3 3.4 %fusion.62 = f32[128,2560]{0,1} fusion(bf16[384,2560]{0,1:T(8,128)(2,1)} %bitcast.97, f32[128,384]{1,0:T(8,128)S(1)} %get-tuple-element.250, f32[128]{0:T(128)S(1)} %add_rsqrt_fusion, f32[384]{0:T(512)S(1)} %copy-done.11), kind=kOutput, calls=%fused_computation.117 | convolution fusion | flops 251805696 | bytes 3475456
  160.7 3.0 %copy.138 = bf16[128,40,64]{2,1,0:T(8,128)(2,1)} copy(f32[128,40,64]{0,2,1:T(8,128)} %bitcast.93) | data formatting | bytes 1966080 | tf_op jit(solution)/shard_map/td,edf->tef/dot_general | solution.py:156
  163.8 10.5 %gather_fusion.2 = bf16[1024,64]{1,0:T(8,128)(2,1)} fusion(bf16[128,40,64]{2,1,0:T(8,128)(2,1)S(1)} %copy.141, s32[1024]{0:T(1024)S(1)} %reshape.431), kind=kCustom, calls=%fused_computation.1.clone | custom fusion | bytes 270336 | tf_op jit(solution)/shard_map/jit(take_along_axis)/gather | solution.py:159
  174.2 12.8 %gather_fusion.1 = bf16[1024,64]{1,0:T(8,128)(2,1)S(1)} fusion(bf16[128,40,64]{2,1,0:T(8,128)(2,1)} %copy.138, s32[1024]{0:T(1024)S(1)} %reshape.431), kind=kCustom, calls=%fused_computation.clone | custom fusion | bytes 270336 | tf_op jit(solution)/shard_map/jit(take_along_axis)/gather | solution.py:158
  188.3 31.8 %all-reduce.6.cloned.1.call-done = (bf16[128,8,64]{2,1,0:T(8,128)(2,1)}, bf16[128,8,64]{2,1,0:T(8,128)(2,1)}) async-done(((bf16[128,8,64]{2,1,0:T(8,128)(2,1)}, bf16[128,8,64]{2,1,0:T(8,128)(2,1)}), (bf16[128,8,64]{2,1,0:T(8,128)(2,1)}, bf16[128,8,64]{2,1,0:T(8,128)(2,1)})) %all-reduce.6.cloned.1.call-update) | async-done | bytes 262160 | tf_op jit(solution)/shard_map/psum | solution.py:162
  220.1 2.5 convolution_convert_fusion
  222.7 1.3 fusion.11
  224.0 70.3 %all-reduce.4.cloned.1.call-done = f32[128,384]{1,0:T(8,128)} async-done(((f32[128,384]{1,0:T(8,128)}), f32[128,384]{1,0:T(8,128)}) %all-reduce.4.cloned.1.call-update) | async-done | bytes 196624 | tf_op jit(solution)/shard_map/psum | solution.py:173
  294.3 1.6 add_convert_fusion
  (129 shorter events, 32.0 us)
Async XLA Ops:
  6.5 146.5 %copy-start = (bf16[40,384,64]{1,2,0:T(8,128)(2,1)S(1)}, bf16[40,384,64]{1,2,0:T(8,128)(2,1)}, u32[]{:S(2)}) copy-start(bf16[40,384,64]{1,2,0:T(8,128)(2,1)} %param.24) | copy-start | bytes 5898244
  6.5 5.4 %copy-start.12 = (s32[32]{0:T(128)S(1)}, s32[32]{0:T(128)}, u32[]{:S(2)}) copy-start(s32[32]{0:T(128)} %param.28) | copy-start | bytes 388
  6.5 94.1 %all-gather.5.cloned.1.call-start = ((), (), s32[]{:S(2)}) async-start(), calls=%async_computation.1 | async-start | bytes 3538944 | tf_op jit(solution)/shard_map/all_gather | solution.py:20
  9.3 3.4 %copy-start.5 = (bf16[32,32,128]{2,1,0:T(8,128)(2,1)S(1)}, bf16[32,32,128]{2,1,0:T(8,128)(2,1)}, u32[]{:S(2)}) copy-start(bf16[32,32,128]{2,1,0:T(8,128)(2,1)} %param.26) | copy-start | bytes 786436
  15.7 1.0 copy-start.7
  15.8 1.0 copy-start.8
  16.8 2.0 copy-start.3
  18.8 1.3 copy-start.1
  18.8 2.7 copy-start.4
  20.0 200.1 %all-reduce.6.cloned.1.call-start = ((), (), s32[]{:S(2)}) async-start(), calls=%async_computation.2 | async-start | bytes 1048576 | tf_op jit(solution)/shard_map/psum | solution.py:162
  22.2 71.0 %copy-start.6 = (s32[128,8]{0,1:T(8,128)S(1)}, s32[128,8]{0,1:T(8,128)}, u32[]{:S(2)}) copy-start(s32[128,8]{0,1:T(8,128)} %param.29) | copy-start | bytes 12292
  119.0 15.8 %copy-start.10 = (bf16[384,40]{0,1:T(8,128)(2,1)S(1)}, bf16[384,40]{0,1:T(8,128)(2,1)}, u32[]{:S(2)}) copy-start(bf16[384,40]{0,1:T(8,128)(2,1)} %param.22) | copy-start | bytes 92164
  119.0 15.8 %copy-start.11 = (f32[384]{0:T(512)S(1)}, f32[384]{0:T(512)}, u32[]{:S(2)}) copy-start(f32[384]{0:T(512)} %param.21) | copy-start | bytes 4612
  174.2 12.9 %copy-start.2 = (bf16[1024,64]{1,0:T(8,128)(2,1)S(1)}, bf16[1024,64]{1,0:T(8,128)(2,1)}, u32[]{:S(2)}) copy-start(bf16[1024,64]{1,0:T(8,128)(2,1)} %gather_fusion.2) | copy-start | bytes 393220
  174.2 45.9 %copy-start.9 = (s32[128,8]{1,0:T(8,128)S(1)}, s32[128,8]{1,0:T(8,128)}, u32[]{:S(2)}) copy-start(s32[128,8]{1,0:T(8,128)} %copy.132) | copy-start | bytes 12292
  188.1 106.2 %all-reduce.4.cloned.1.call-start = ((), (), s32[]{:S(2)}) async-start(), calls=%async_computation | async-start | bytes 393216 | tf_op jit(solution)/shard_map/psum | solution.py:173
  220.1 2.6 copy-start.13
Sparse Core Ops, SparseCore 0:
  20.1 80.4 all-gather.4
  188.2 31.8 all-reduce.5
  224.1 70.1 all-reduce.3
where the time goes:
time: 303 us; the launch traced here: 302 us
  waiting for transfers between devices  108 us (36%)
  blocking collectives  93.5 us (31%)
  local copies, waits for them, and re-layouts  53.4 us (18%)
  matrix products  17.4 us (6%)
  other arithmetic  15.7 us (5%)
  between operations  13.5 us (4%)
    psum x1, waiting for transfers between devices, on_device(): moe_out = lax.psum(moe_part, 'seq')  70.3 us
    all_gather x2, blocking collectives, joined(): everything = jax.tree.map(lambda part: lax.all_gather(part, axis), shard)  69.6 us
    psum x1, waiting for transfers between devices, on_device(): lax.psum(up_pick.astype(jnp.bfloat16), 'tp').astype(jnp.float32)  31.8 us
    gather x3, local copies, waits for them, and re-layouts, on_device(): gate_pick = jnp.take_along_axis(gate_part, routes[:, :, None], axis=1)  13 us
    psum x1, blocking collectives, on_device(): lax.psum(jnp.dot(gained * scale[:, None], router_f, precision=lax.Precisi...  10.7 us
    gather x1, local copies, waits for them, and re-layouts, on_device(): up_pick = jnp.take_along_axis(up_part, routes[:, :, None], axis=1)  10.5 us
    gather x5, local copies, waits for them, and re-layouts, on_device(): chosen = jnp.take_along_axis(logits, routes, axis=1)  7.34 us
    dynamic_slice x7, local copies, waits for them, and re-layouts, lap(): return combine(so_far, jax.tree.map(lambda part: part[k], everything))  7.3 us
  transfers between devices with their start and end apart: 3, of which 3 were waited for; matrix products, arithmetic and copies ran while one was open for 2% of the time, Pallas kernels for 0%

commit v1 on v0

--- a/solution.py
+++ b/solution.py
@@ -1,6 +1,8 @@
 import jax
 import jax.numpy as jnp
 from jax import lax
+from jax.experimental import pallas as pl
+from jax.experimental.pallas import tpu as pltpu
 from jax.sharding import PartitionSpec as P
 
 D = 1536
@@ -174,6 +176,517 @@
     return (residual + moe_out).astype(jnp.bfloat16)
 
 
+TOP = 8
+TILE = 16
+LANES = 128
+SEQ = 8
+TP = 4
+MESH = pl.DeviceIdType.MESH
+
+
+def fits_fused(mesh):
+    return mesh.shape["seq"] == SEQ and mesh.shape["tp"] == TP
+
+
+def lane_of(shape):
+    return lax.broadcasted_iota(jnp.int32, shape, len(shape) - 1)
+
+
+def swap_half(values):
+    return pltpu.roll(values, 64, 1)
+
+
+def split_pair(values):
+    high = values.astype(jnp.bfloat16).astype(jnp.float32)
+    return jnp.where(lane_of(values.shape) < 64, high, values - high).astype(jnp.bfloat16)
+
+
+def join_pair(packed):
+    values = packed.astype(jnp.float32)
+    return values + swap_half(values)
+
+
+def layer_kernel(
+    tokens_ref,
+    attn_gain_ref,
+    moe_gain_ref,
+    cos_ref,
+    sin_ref,
+    bias_ref,
+    routes_ref,
+    router_ref,
+    qkv_hbm,
+    keys_hbm,
+    values_hbm,
+    out_w_hbm,
+    gate_hbm,
+    up_hbm,
+    down_hbm,
+    out_ref,
+    qkv_ref,
+    keys_ref,
+    values_ref,
+    out_w_ref,
+    gate_ref,
+    up_ref,
+    down_ref,
+    att_send,
+    att_recv,
+    att_all,
+    res_own,
+    res_all,
+    pair_w,
+    dense,
+    onehot,
+    shifted,
+    picks,
+    picks_recv,
+    picks_half,
+    picks_far,
+    logit_rows,
+    scaled,
+    scaled_f,
+    total,
+    part_send,
+    part_recv,
+    out_own,
+    local_sem,
+    seq_send,
+    seq_recv,
+    tp_send,
+    tp_recv,
+):
+    me = lax.axis_index("seq")
+    tp = lax.axis_index("tp")
+    core = lax.rem(tp, 2)
+    core_peer = tp + 1 - 2 * core
+    far_peer = lax.rem(tp + 2, TP)
+    f32, bf16 = jnp.float32, jnp.bfloat16
+
+    barrier = pltpu.get_barrier_semaphore()
+    for step in range(1, SEQ):
+        pl.semaphore_signal(
+            barrier, inc=1, device_id=(lax.rem(me + step, SEQ), tp), device_id_type=MESH
+        )
+    for step in range(1, TP):
+        pl.semaphore_signal(
+            barrier, inc=1, device_id=(me, lax.rem(tp + step, TP)), device_id_type=MESH
+        )
+
+    loads = [
+        pltpu.make_async_copy(src, dst, local_sem.at[n])
+        for n, (src, dst) in enumerate(
+            [
+                (qkv_hbm, qkv_ref),
+                (keys_hbm, keys_ref),
+                (values_hbm, values_ref),
+                (gate_hbm, gate_ref),
+                (up_hbm, up_ref),
+                (out_w_hbm, out_w_ref),
+                (down_hbm, down_ref),
+            ]
+        )
+    ]
+    for load in loads:
+        load.start()
+
+    def seq_copies(phase, source, target):
+        copies = []
+        for step in range(1, SEQ):
+            peer = lax.rem(me + step, SEQ)
+            copies.append(
+                pltpu.make_async_remote_copy(
+                    src_ref=source(peer),
+                    dst_ref=target(me),
+                    send_sem=seq_send.at[phase, step],
+                    recv_sem=seq_recv.at[phase, step],
+                    device_id=(peer, tp),
+                    device_id_type=MESH,
+                )
+            )
+        for copy in copies:
+            copy.start()
+        return copies
+
+    def tp_copy(slot, source, target, peer):
+        copy = pltpu.make_async_remote_copy(
+            src_ref=source,
+            dst_ref=target,
+            send_sem=tp_send.at[slot],
+            recv_sem=tp_recv.at[slot],
+            device_id=(me, peer),
+            device_id_type=MESH,
+        )
+        copy.start()
+        return copy
+
+    def rows_of(index):
+        return pl.ds(pl.multiple_of(index * TILE, TILE), TILE)
+
+    token_full = tokens_ref[...].astype(f32)
+    normed = rms_scale(token_full, attn_gain_ref[...]).astype(bf16)
+    loads[0].wait()
+    projected = jnp.dot(normed, qkv_ref[...], preferred_element_type=f32)
+    tiles = [projected[:, LANES * n : LANES * (n + 1)] for n in range(5)]
+    lane = lane_of(tiles[0].shape)
+    low = lane < 64
+    cosine, sine = cos_ref[...], sin_ref[...]
+
+    def turned(x):
+        swapped = jnp.where(lane % 64 < 32, pltpu.roll(x, 96, 1), pltpu.roll(x, 32, 1))
+        return x * cosine + swapped * sine
+
+    turn = [turned(x) for x in tiles]
+    factor = 1.0 / HEAD**0.5
+    queries = [
+        jnp.where(low, turn[0], 0.0),
+        jnp.where(low, swap_half(turn[0]), 0.0),
+        jnp.where(low, turn[1], 0.0),
+        jnp.where(low, 0.0, turn[2]),
+        jnp.where(low, 0.0, swap_half(turn[3])),
+        jnp.where(low, 0.0, turn[3]),
+    ]
+    queries = [(q * factor).astype(bf16) for q in queries]
+    new_keys = jnp.where(low, swap_half(turn[1]), swap_half(turn[4])).astype(bf16)
+    new_values = jnp.where(low, tiles[2], tiles[4]).astype(bf16)
+
+    loads[1].wait()
+    loads[2].wait()
+    row32 = lax.broadcasted_iota(jnp.int32, (32, 32), 0)
+    col32 = lax.broadcasted_iota(jnp.int32, (32, 32), 1)
+    own = (row32 // NEW == col32 // NEW) & (col32 <= row32) & (me == 0)
+    own_bias = jnp.where(own, 0.0, FLOOR_SCORE).astype(f32)
+    own_bias = jnp.concatenate([own_bias] * 6, axis=0)
+    contract = (((1,), (1,)), ((), ()))
+    for block in range(4):
+        at = slice(32 * block, 32 * block + 32)
+        slots = slice(256 * block, 256 * block + 256)
+        query = jnp.concatenate([q[at] for q in queries], axis=0)
+        old_bias = jnp.concatenate([bias_ref[at, :]] * 6, axis=0)
+        old = lax.dot_general(query, keys_ref[slots, :], contract, preferred_element_type=f32)
+        new = lax.dot_general(query, new_keys[at], contract, preferred_element_type=f32)
+        old = old + old_bias
+        new = new + own_bias
+        top = jnp.maximum(
+            jnp.max(old, axis=-1, keepdims=True), jnp.max(new, axis=-1, keepdims=True)
+        )
+        old = jnp.exp(old - top)
+        new = jnp.exp(new - top)
+        mass = jnp.sum(old, axis=-1, keepdims=True) + jnp.sum(new, axis=-1, keepdims=True)
+        mixed = jnp.dot(
+            old.astype(bf16), values_ref[slots, :], preferred_element_type=f32
+        ) + jnp.dot(new.astype(bf16), new_values[at], preferred_element_type=f32)
+        mixed = mixed / mass
+        level = top + jnp.log(mass)
+        head = [mixed[32 * n : 32 * n + 32] for n in range(6)]
+        lane32 = lane_of((32, LANES))
+        low32 = lane32 < 64
+        att_send[at, 0:128] = jnp.where(low32, head[0], swap_half(head[1])).astype(bf16)
+        att_send[at, 128:256] = jnp.where(low32, head[2], head[3]).astype(bf16)
+        att_send[at, 256:384] = jnp.where(low32, swap_half(head[4]), head[5]).astype(bf16)
+        levels = jnp.zeros((32, LANES), f32)
+        for n in range(6):
+            levels = jnp.where(lane32 % 8 == n, level[32 * n : 32 * n + 32], levels)
+        high = levels.astype(bf16).astype(f32)
+        rest = levels - high
+        middle = rest.astype(bf16).astype(f32)
+        levels = jnp.where(
+            lane32 < 8, high, jnp.where(lane32 < 16, middle, rest - middle)
+        )
+        att_send[at, 384:512] = jnp.where(lane32 < 24, levels, 0.0).astype(bf16)
+
+    pl.semaphore_wait(barrier, SEQ + TP - 2)
+    copies = seq_copies(
+        0, lambda peer: att_send.at[rows_of(peer), :], lambda index: att_recv.at[index]
+    )
+    att_recv[me] = att_send[rows_of(me), :]
+
+    loads[3].wait()
+    loads[4].wait()
+
+    def pack(n, carry):
+        pair_w[n] = jnp.concatenate(
+            [gate_ref[2 * n], up_ref[2 * n], gate_ref[2 * n + 1], up_ref[2 * n + 1]], axis=-1
+        )
+        return carry
+
+    lax.fori_loop(0, EXPERTS // 2, pack, 0)
+    spread_col = lax.broadcasted_iota(jnp.int32, (TILE, EXPERTS * TILE), 1)
+    spread_row = lax.broadcasted_iota(jnp.int32, (TILE, EXPERTS * TILE), 0)
+    expert_at = jnp.where(spread_col % TILE == spread_row, spread_col // TILE, -1)
+
+    def mark(n, carry):
+        routes = routes_ref[rows_of(n), :]
+        for k in range(TOP):
+            hit = routes[:, k : k + 1] == expert_at
+            onehot[n, TILE * k : TILE * (k + 1), :] = jnp.where(hit, 1.0, 0.0).astype(bf16)
+        return carry
+
+    lax.fori_loop(0, 8, mark, 0)
+    half_lane = jnp.where(low, 0, 1)
+    for k in range(TOP):
+        shifted[k] = routes_ref[:, k : k + 1] - half_lane
+
+    for copy in copies:
+        copy.wait()
+    own_level = []
+    for n in range(SEQ):
+        packed = att_recv[n, :, 384:512].astype(f32)
+        own_level.append(packed + pltpu.roll(packed, 120, 1) + pltpu.roll(packed, 112, 1))
+    top = own_level[0]
+    for n in range(1, SEQ):
+        top = jnp.maximum(top, own_level[n])
+    weights = [jnp.exp(x - top) for x in own_level]
+    mass = weights[0]
+    for n in range(1, SEQ):
+        mass = mass + weights[n]
+    low16 = lane_of((TILE, LANES)) < 64
+    parts = [jnp.zeros((TILE, LANES), f32) for _ in range(3)]
+    for n in range(SEQ):
+        share = weights[n] / mass
+        for j in range(3):
+            wide = jnp.where(low16, share[:, 2 * j : 2 * j + 1], share[:, 2 * j + 1 : 2 * j + 2])
+            parts[j] = parts[j] + wide * att_recv[n, :, 128 * j : 128 * j + 128].astype(f32)
+    att_all[tp] = jnp.concatenate(parts, axis=-1).astype(bf16)
+
+    copies = [
+        tp_copy(step, att_all.at[tp], att_all.at[tp], lax.rem(tp + step, TP))
+        for step in range(1, TP)
+    ]
+    loads[5].wait()
+    width = out_w_ref.shape[1]
+    residual = tokens_ref[rows_of(me), pl.ds(pl.multiple_of(tp * width, 128), width)].astype(f32)
+    for copy in copies:
+        copy.wait()
+    for n in range(TP):
+        residual = residual + jnp.dot(
+            att_all[n], out_w_ref[width * n : width * (n + 1), :], preferred_element_type=f32
+        )
+    res_own[...] = residual
+    res_all[me] = residual.astype(bf16)
+    copies = seq_copies(1, lambda peer: res_all.at[me], lambda index: res_all.at[index])
+    for copy in copies:
+        copy.wait()
+
+    full = res_all[...].reshape(SEQ * TILE, width).astype(f32)
+    gained = full * moe_gain_ref[...]
+    gained_b = gained.astype(bf16)
+    rest = (gained - gained_b.astype(f32)).astype(bf16)
+    router = router_ref[...]
+    logits = jnp.dot(gained_b, router, preferred_element_type=f32) + jnp.dot(
+        rest, router, preferred_element_type=f32
+    )
+    squares = jnp.sum(full * full, axis=-1, keepdims=True)
+    logit_rows[...] = jnp.zeros_like(logit_rows)
+    logit_rows[:, 0:EXPERTS] = logits
+    rows = jnp.where(lane == EXPERTS, squares, logit_rows[...])
+    rows = split_pair(jnp.where(low, rows, swap_half(rows)))
+    picks[:, TOP * TILE :, :] = rows.reshape(8, TILE, LANES)
+
+    def experts(n, carry):
+        both = jnp.dot(gained_b, pair_w[n], preferred_element_type=f32).astype(bf16)
+        dense[2 * n] = both[:, :LANES]
+        dense[2 * n + 1] = both[:, LANES:]
+        return carry
+
+    lax.fori_loop(0, EXPERTS // 2, experts, 0)
+
+    def pick(n, carry):
+        group = dense[:, rows_of(n), :].reshape(EXPERTS * TILE, LANES)
+        picks[n, 0 : TOP * TILE, :] = jnp.dot(
+            onehot[n], group, preferred_element_type=f32
+        ).astype(bf16)
+        return carry
+
+    lax.fori_loop(0, 8, pick, 0)
+
+    mine = pl.ds(4 * core, 4)
+    copy = tp_copy(4, picks.at[pl.ds(4 * (1 - core), 4)], picks_recv, core_peer)
+    copy.wait()
+    picks_half[:, 0 : TOP * TILE, :] = (
+        picks[mine, 0 : TOP * TILE, :].astype(f32) + picks_recv[:, 0 : TOP * TILE, :].astype(f32)
+    ).astype(bf16)
+    ours = picks[mine, TOP * TILE :, :].reshape(64, LANES)
+    theirs = picks_recv[:, TOP * TILE :, :].reshape(64, LANES)
+    picks_half[:, TOP * TILE :, :] = split_pair(join_pair(ours) + join_pair(theirs)).reshape(
+        4, TILE, LANES
+    )
+    copy = tp_copy(5, picks_half, picks_far, far_peer)
+    copy.wait()
+    rows = join_pair(picks_half[:, TOP * TILE :, :].reshape(64, LANES)) + join_pair(
+        picks_far[:, TOP * TILE :, :].reshape(64, LANES)
+    )
+    lane64 = lane_of((64, LANES))
+    low64 = lane64 < 64
+    scale = lax.rsqrt(rows[:, EXPERTS : EXPERTS + 1] / D + EPSILON)
+    routes = routes_ref[pl.ds(pl.multiple_of(64 * core, 64), 64), :]
+    hits = [lane64 == routes[:, k : k + 1] for k in range(TOP)]
+    routed = hits[0]
+    for k in range(1, TOP):
+        routed = routed | hits[k]
+    scores = jnp.where(routed, rows * scale, FLOOR_SCORE)
+    prob = jnp.exp(scores - jnp.max(scores, axis=-1, keepdims=True))
+    prob = jnp.where(routed, prob, 0.0)
+    prob = prob / jnp.sum(prob, axis=-1, keepdims=True)
+    for k in range(TOP):
+        at = slice(TILE * k, TILE * (k + 1))
+        both = (picks_half[:, at, :].astype(f32) + picks_far[:, at, :].astype(f32)).reshape(
+            64, LANES
+        ) * scale
+        active = both / (1.0 + jnp.exp(-both)) * swap_half(both)
+        active = active.astype(bf16).astype(f32)
+        active = active * jnp.sum(jnp.where(hits[k], prob, 0.0), axis=-1, keepdims=True)
+        active = jnp.where(low64, active, swap_half(active))
+        scaled[mine, at, :] = active.astype(bf16).reshape(4, TILE, LANES)
+    copy = tp_copy(6, scaled.at[mine], scaled.at[mine], core_peer)
+    loads[6].wait()
+    copy.wait()
+
+    for k in range(TOP):
+        scaled_f[k] = scaled[:, TILE * k : TILE * (k + 1), :].reshape(128, LANES).astype(f32)
+    total[...] = jnp.zeros_like(total)
+
+    def down(n, carry):
+        spread = []
+        for pair in range(2):
+            wanted = 4 * n + 2 * pair
+            one = jnp.zeros((128, LANES), f32)
+            for k in range(TOP):
+                one = jnp.where(shifted[k] == wanted, scaled_f[k], one)
+            spread.append(one)
+        spread = jnp.concatenate(spread, axis=-1).astype(bf16)
+        weight = down_ref[pl.ds(4 * n, 4)].reshape(256, width)
+        total[...] += jnp.dot(spread, weight, preferred_element_type=f32)
+        return carry
+
+    lax.fori_loop(0, EXPERTS // 4, down, 0)
+    part_send[...] = total[...].astype(bf16)
+
+    copies = seq_copies(
+        2, lambda peer: part_send.at[rows_of(peer), :], lambda index: part_recv.at[index]
+    )
+    result = res_own[...] + total[rows_of(me), :]
+    for copy in copies:
+        copy.wait()
+    part_recv[me] = jnp.zeros((TILE, width), bf16)
+    for n in range(SEQ):
+        result = result + part_recv[n].astype(f32)
+    out_own[...] = result.astype(bf16)
+    out_ref[rows_of(me), :] = out_own[...]
+    copies = seq_copies(3, lambda peer: out_own, lambda index: out_ref.at[rows_of(index), :])
+    for copy in copies:
+        copy.wait()
+
+
+def fused_device(
+    tokens,
+    attn_gain,
+    qkv_weight,
+    out_weight,
+    moe_gain,
+    router_weight,
+    expert_gate,
+    expert_up,
+    expert_down,
+    cache_keys,
+    cache_values,
+    lengths,
+    routes,
+):
+    seq_index = lax.axis_index("seq")
+    count = tokens.shape[0]
+    width = out_weight.shape[1]
+    requests, slot_count = cache_keys.shape[:2]
+    window = slot_count * SEQ - SINK
+    places = (
+        (lengths[:, None] + jnp.arange(NEW, dtype=jnp.int32)[None, :])
+        .reshape(count)
+        .astype(jnp.float32)
+    )
+    lane = jnp.arange(LANES, dtype=jnp.int32)
+    half = HEAD // 2
+    freqs = jnp.exp(-jnp.log(ROPE_BASE) * (lane % half).astype(jnp.float32) / half)
+    angles = places[:, None] * freqs[None, :]
+    cosine = jnp.cos(angles)
+    sine = jnp.where((lane % HEAD < half)[None, :], -jnp.sin(angles), jnp.sin(angles))
+    column = jnp.arange(8 * slot_count, dtype=jnp.int32)
+    token = jnp.arange(count, dtype=jnp.int32)
+    lens = jnp.repeat(lengths, NEW)[:, None]
+    slot = (seq_index * slot_count + column % slot_count)[None, :]
+    older = lens - 1 - jnp.mod(lens - 1 - slot, window)
+    seen = (slot < lens) & ((slot < SINK) | (older >= lens + (token % NEW)[:, None] - window))
+    same = ((token // NEW) % 8)[:, None] == (column // slot_count)[None, :]
+    bias = jnp.where(seen & same, 0.0, FLOOR_SCORE).astype(jnp.float32)
+
+    vmem = pl.BlockSpec(memory_space=pltpu.VMEM)
+    anywhere = pl.BlockSpec(memory_space=pl.ANY)
+    bf16, f32 = jnp.bfloat16, jnp.float32
+    hidden = expert_gate.shape[2]
+    return pl.pallas_call(
+        layer_kernel,
+        out_shape=jax.ShapeDtypeStruct((count, width), bf16),
+        in_specs=[vmem] * 8 + [anywhere] * 7,
+        out_specs=vmem,
+        scratch_shapes=[
+            pltpu.VMEM(qkv_weight.shape, bf16),
+            pltpu.VMEM((requests * slot_count, LANES), bf16),
+            pltpu.VMEM((requests * slot_count, LANES), bf16),
+            pltpu.VMEM(out_weight.shape, bf16),
+            pltpu.VMEM(expert_gate.shape, bf16),
+            pltpu.VMEM(expert_up.shape, bf16),
+            pltpu.VMEM(expert_down.shape, bf16),
+            pltpu.VMEM((count, 512), bf16),
+            pltpu.VMEM((SEQ, TILE, 512), bf16),
+            pltpu.VMEM((TP, TILE, width), bf16),
+            pltpu.VMEM((TILE, width), f32),
+            pltpu.VMEM((SEQ, TILE, width), bf16),
+            pltpu.VMEM((EXPERTS // 2, width, 4 * hidden), bf16),
+            pltpu.VMEM((EXPERTS, count, LANES), bf16),
+            pltpu.VMEM((8, TOP * TILE, EXPERTS * TILE), bf16),
+            pltpu.VMEM((TOP, count, LANES), jnp.int32),
+            pltpu.VMEM((8, (TOP + 1) * TILE, LANES), bf16),
+            pltpu.VMEM((4, (TOP + 1) * TILE, LANES), bf16),
+            pltpu.VMEM((4, (TOP + 1) * TILE, LANES), bf16),
+            pltpu.VMEM((4, (TOP + 1) * TILE, LANES), bf16),
+            pltpu.VMEM((count, LANES), f32),
+            pltpu.VMEM((8, TOP * TILE, LANES), bf16),
+            pltpu.VMEM((TOP, count, LANES), f32),
+            pltpu.VMEM((count, width), f32),
+            pltpu.VMEM((count, width), bf16),
+            pltpu.VMEM((SEQ, TILE, width), bf16),
+            pltpu.VMEM((TILE, width), bf16),
+            pltpu.SemaphoreType.DMA((7,)),
+            pltpu.SemaphoreType.DMA((4, SEQ)),
+            pltpu.SemaphoreType.DMA((4, SEQ)),
+            pltpu.SemaphoreType.DMA((7,)),
+            pltpu.SemaphoreType.DMA((7,)),
+        ],
+        compiler_params=pltpu.CompilerParams(
+            collective_id=0, has_side_effects=True, vmem_limit_bytes=48 * 1024 * 1024
+        ),
+        cost_estimate=pl.CostEstimate(
+            flops=2_000_000_000, bytes_accessed=20_000_000, transcendentals=1_000_000
+        ),
+        name="layer",
+    )(
+        tokens,
+        attn_gain.reshape(1, -1),
+        moe_gain.reshape(1, -1),
+        cosine,
+        sine,
+        bias,
+        routes,
+        router_weight,
+        qkv_weight,
+        cache_keys.reshape(-1, LANES),
+        cache_values.reshape(-1, LANES),
+        out_weight,
+        expert_gate,
+        expert_up,
+        expert_down,
+    )
+
+
 def solution(mesh):
     in_specs = (
         P(),
@@ -191,6 +704,7 @@
         P(),
     )
     out_specs = P(None, "tp")
+    body = fused_device if fits_fused(mesh) else on_device
     return jax.shard_map(
-        on_device, mesh=mesh, in_specs=in_specs, out_specs=out_specs, check_vma=False
-    )
+        body, mesh=mesh, in_specs=in_specs, out_specs=out_specs, check_vma=False
+    )

time: 303 us -> 64.4 us (0.21)
  waiting for transfers between devices: 108 us -> 0 us
  blocking collectives: 93.5 us -> 0 us
  Pallas kernels: 0 us -> 44.7 us
  local copies, waits for them, and re-layouts: 53.4 us -> 17.9 us
  matrix products: 17.4 us -> 0 us
  other arithmetic: 15.7 us -> 1.18 us
  between operations: 13.5 us -> 0.06 us
    psum x2 -> x0, waiting for transfers between devices: 102 us -> none  [the longest x1 70.3 us: on_device(): moe_out = lax.psum(moe_part, 'seq')]
    all_gather x3 -> x0, blocking collectives: 76 us -> none  [the longest x2 69.6 us: joined(): everything = jax.tree.map(lambda part: lax.all_gather(part, axis), shard)]
    pallas_call x0 -> x1, Pallas kernels: none -> 44.7 us  [fused_device(): pl.pallas_call(layer_kernel, out_shape=jax.ShapeDtypeStruct((count, width...]
    gather x9 -> x0, local copies, waits for them, and re-layouts: 30.8 us -> none  [the longest x3 13 us: on_device(): gate_pick = jnp.take_along_axis(gate_part, routes[:, :, None], axis=1)]
    psum x2 -> x0, blocking collectives: 17.5 us -> none  [the longest x1 10.7 us: on_device(): lax.psum(jnp.dot(gained * scale[:, None], router_f, precision=lax.Precisi...]
    unnamed x29 -> x17, local copies, waits for them, and re-layouts: 0.8 us -> 15.6 us
    dot_general x9 -> x0, matrix products: 12.2 us -> none  [the longest x1 2.64 us: on_device(): projected = jnp.dot(normed, qkv_weight, preferred_element_type=jnp.float32)]
    add x16 -> x0, other arithmetic: 8.1 us -> none  [the longest x7 6.97 us: combine_parts(): weighted_a * factor_a[..., None] + weighted_b * factor_b[..., None]]
  transfers between devices with their start and end apart: 3 -> 0, of which waited for: 3 -> 0; matrix products, arithmetic and copies ran while one was open for 2% -> 0% of each run, Pallas kernels for 0% -> 0%
where the time goes in v1:
time: 64.4 us; the launch traced here: 63.9 us
  Pallas kernels  44.7 us (69%)
  local copies, waits for them, and re-layouts  17.9 us (28%)
  other arithmetic  1.18 us (2%)
    pallas_call x1, Pallas kernels, fused_device(): pl.pallas_call(layer_kernel, out_shape=jax.ShapeDtypeStruct((count, width...  44.7 us
    unnamed x17, local copies, waits for them, and re-layouts  15.6 us

profile of v1, /device:TPU:0, one launch (start us, length us, event | category | flops | bytes accessed | tf_op | source)
XLA Modules:
  0.0 63.9 jit_solution(2940754057454180007)
XLA Ops:
  0.0 0.7 %reshape.126.moe_gain_ref = f32[1,384]{1,0:T(1,128)S(1)} reshape(f32[384]{0:T(512)} %param.17) | data formatting | bytes 3072 | tf_op jit(solution)/shard_map/reshape | solution.py:674
  0.7 0.7 %reshape.125.attn_gain_ref = f32[1,1536]{1,0:T(1,128)S(1)} reshape(f32[1536]{0:T(1024)} %param.14) | data formatting | bytes 12288 | tf_op jit(solution)/shard_map/reshape | solution.py:673
  1.4 0.7 %add.118 = s32[32,4]{1,0:T(8,128)S(1)} broadcast(s32[32]{0:T(128)} %param.24), dimensions={0} | broadcast | bytes 640 | tf_op jit(solution)/shard_map/add | solution.py:602
  2.1 0.1 add.119
  2.3 0.1 add.121
  2.4 0.8 %copy.18.routes_ref = s32[128,8]{1,0:T(8,128)S(1)} copy(s32[128,8]{0,1:T(8,128)} %param.25) | data formatting | bytes 8192 | tf_op args[12]
  3.2 0.9 %copy.19.router_ref = bf16[384,40]{1,0:T(8,128)(2,1)S(1)} copy(bf16[384,40]{0,1:T(8,128)(2,1)} %param.18) | data formatting | bytes 61440 | tf_op args[5]
  4.0 0.2 fusion.8.bias_ref
  4.3 0.9 %negate_select_fusion = (f32[128,128]{1,0:T(8,128)S(1)}, f32[128,128]{1,0:T(8,128)}) fusion(f32[128]{0:T(128)S(1)} %fusion.14, f32[128]{0:T(128)S(1)} %get-tuple-element.9, pred[128]{0:T(512)(128)(4,1)S(1)} %fusion.15), kind=kLoop, calls=%fused_computation.11 | loop fusion | flops 49152 | bytes 132224 | tf_op jit(solution)/shard_map/jit(_where)/select_n | solution.py:611
  5.2 4.7 %copy.20.gate_hbm = bf16[40,384,64]{2,1,0:T(8,128)(2,1)} copy(bf16[40,384,64]{1,2,0:T(8,128)(2,1)} %param.19) | data formatting | bytes 3932160 | tf_op args[6]
  9.9 0.0 copy-start
  9.9 0.0 copy-start.1
  9.9 4.8 %copy.21.up_hbm = bf16[40,384,64]{2,1,0:T(8,128)(2,1)} copy(bf16[40,384,64]{1,2,0:T(8,128)(2,1)} %param.20) | data formatting | bytes 3932160 | tf_op args[7]
  14.7 0.0 copy-done
  14.7 0.0 copy-done.1
  14.7 0.0 copy-start.2
  14.7 1.0 %copy-done.2 = bf16[128,1536]{1,0:T(8,128)(2,1)S(1)} copy-done((bf16[128,1536]{1,0:T(8,128)(2,1)S(1)}, bf16[128,1536]{1,0:T(8,128)(2,1)}, u32[]{:S(2)}) %copy-start.2) | copy-done | bytes 393240
  15.7 0.0 copy-start.3
  15.7 0.9 %copy-done.3 = bf16[32,32,128]{2,1,0:T(8,128)(2,1)S(1)} copy-done((bf16[32,32,128]{2,1,0:T(8,128)(2,1)S(1)}, bf16[32,32,128]{2,1,0:T(8,128)(2,1)}, u32[]{:S(2)}) %copy-start.3) | copy-done | bytes 262168
  16.7 0.0 copy-start.4
  16.7 0.9 %copy-done.4 = bf16[32,32,128]{2,1,0:T(8,128)(2,1)S(1)} copy-done((bf16[32,32,128]{2,1,0:T(8,128)(2,1)S(1)}, bf16[32,32,128]{2,1,0:T(8,128)(2,1)}, u32[]{:S(2)}) %copy-start.4) | copy-done | bytes 262168
  17.6 0.8 %copy-done.5 = f32[128,128]{1,0:T(8,128)S(1)} copy-done((f32[128,128]{1,0:T(8,128)S(1)}, f32[128,128]{1,0:T(8,128)}, u32[]{:S(2)}) %copy-start.5) | copy-done | bytes 65560
  18.5 44.7 %layer.1 = bf16[128,384]{1,0:T(8,128)(2,1)S(1)} custom-call(bf16[128,1536]{1,0:T(8,128)(2,1)S(1)} %copy-done.2, f32[1,1536]{1,0:T(1,128)S(1)} %reshape.125.attn_gain_ref, f32[1,384]{1,0:T(1,128)S(1)} %reshape.126.moe_gain_ref, f32[128,128]{1,0:T(8,128)S(1)} %copy-done.5, f32[128,128]{1,0:T(8,128)S(1)} %get-tuple-element.5.sin_ref, ...), custom_call_target="tpu_custom_call" | custom-call | flops 2000000000 | bytes 20000000 | tf_op jit(solution)/shard_map/layer/pallas_call | solution.py:625
  63.2 0.6 %copy.23 = bf16[128,384]{1,0:T(8,128)(2,1)} copy(bf16[128,384]{1,0:T(8,128)(2,1)S(1)} %layer.1) | data formatting | bytes 196608
  (7 shorter events, 0.0 us)
Async XLA Ops:
  9.9 4.8 %copy-start = (bf16[1536,640]{1,0:T(8,128)(2,1)S(1)}, bf16[1536,640]{1,0:T(8,128)(2,1)}, u32[]{:S(2)}) copy-start(bf16[1536,640]{1,0:T(8,128)(2,1)} %qkv_hbm.1) | copy-start | bytes 5898244
  9.9 4.8 %copy-start.1 = (bf16[1536,384]{1,0:T(8,128)(2,1)S(1)}, bf16[1536,384]{1,0:T(8,128)(2,1)}, u32[]{:S(2)}) copy-start(bf16[1536,384]{1,0:T(8,128)(2,1)} %out_w_hbm.1) | copy-start | bytes 3538948
  14.7 1.0 %copy-start.2 = (bf16[128,1536]{1,0:T(8,128)(2,1)S(1)}, bf16[128,1536]{1,0:T(8,128)(2,1)}, u32[]{:S(2)}) copy-start(bf16[128,1536]{1,0:T(8,128)(2,1)} %tokens_ref.1) | copy-start | bytes 1179652
  15.7 0.9 %copy-start.3 = (bf16[32,32,128]{2,1,0:T(8,128)(2,1)S(1)}, bf16[32,32,128]{2,1,0:T(8,128)(2,1)}, u32[]{:S(2)}) copy-start(bf16[32,32,128]{2,1,0:T(8,128)(2,1)} %param.22) | copy-start | bytes 786436
  16.7 0.9 %copy-start.4 = (bf16[32,32,128]{2,1,0:T(8,128)(2,1)S(1)}, bf16[32,32,128]{2,1,0:T(8,128)(2,1)}, u32[]{:S(2)}) copy-start(bf16[32,32,128]{2,1,0:T(8,128)(2,1)} %param.23) | copy-start | bytes 786436
  17.6 0.8 %copy-start.5 = (f32[128,128]{1,0:T(8,128)S(1)}, f32[128,128]{1,0:T(8,128)}, u32[]{:S(2)}) copy-start(f32[128,128]{1,0:T(8,128)} %get-tuple-element.6.cos_ref) | copy-start | bytes 196612

commit v2 on v1

--- a/solution.py
+++ b/solution.py
@@ -1,5 +1,6 @@
 import jax
 import jax.numpy as jnp
+import numpy as np
 from jax import lax
 from jax.experimental import pallas as pl
 from jax.experimental.pallas import tpu as pltpu
@@ -182,6 +183,11 @@
 SEQ = 8
 TP = 4
 MESH = pl.DeviceIdType.MESH
+CHUNKS = 2
+VMEM_LIMIT = 62 * 1024 * 1024
+TURN = 6.28125
+TURN_MIDDLE = 0.0019350051879882812
+TURN_REST = 3.0199159819568123e-07
 
 
 def fits_fused(mesh):
@@ -207,14 +213,12 @@
 
 
 def layer_kernel(
-    tokens_ref,
-    attn_gain_ref,
-    moe_gain_ref,
-    cos_ref,
-    sin_ref,
-    bias_ref,
-    routes_ref,
-    router_ref,
+    tokens_hbm,
+    attn_gain_hbm,
+    moe_gain_hbm,
+    lengths_hbm,
+    routes_hbm,
+    router_hbm,
     qkv_hbm,
     keys_hbm,
     values_hbm,
@@ -223,12 +227,17 @@
     up_hbm,
     down_hbm,
     out_ref,
+    tokens_ref,
+    attn_gain_ref,
+    moe_gain_ref,
+    lengths_ref,
+    routes_t_ref,
+    router_ref,
+    routes_ref,
     qkv_ref,
     keys_ref,
     values_ref,
     out_w_ref,
-    gate_ref,
-    up_ref,
     down_ref,
     att_send,
     att_recv,
@@ -273,21 +282,29 @@
             barrier, inc=1, device_id=(me, lax.rem(tp + step, TP)), device_id_type=MESH
         )
 
+    depth = qkv_ref.shape[0] // 3
+    hidden = gate_hbm.shape[1]
+    wanted = [
+        (lengths_hbm, lengths_ref),
+        (tokens_hbm, tokens_ref),
+        (attn_gain_hbm, attn_gain_ref),
+        (qkv_hbm.at[0:depth], qkv_ref.at[0:depth]),
+        (qkv_hbm.at[depth : 2 * depth], qkv_ref.at[depth : 2 * depth]),
+        (qkv_hbm.at[2 * depth :], qkv_ref.at[2 * depth :]),
+        (keys_hbm, keys_ref),
+        (values_hbm, values_ref),
+        (routes_hbm, routes_t_ref),
+        (moe_gain_hbm, moe_gain_ref),
+        (router_hbm, router_ref),
+        (out_w_hbm, out_w_ref),
+        (gate_hbm, pair_w.at[:, 0:hidden, :]),
+        (up_hbm, pair_w.at[:, hidden:, :]),
+        (down_hbm, down_ref),
+    ]
     loads = [
-        pltpu.make_async_copy(src, dst, local_sem.at[n])
-        for n, (src, dst) in enumerate(
-            [
-                (qkv_hbm, qkv_ref),
-                (keys_hbm, keys_ref),
-                (values_hbm, values_ref),
-                (gate_hbm, gate_ref),
-                (up_hbm, up_ref),
-                (out_w_hbm, out_w_ref),
-                (down_hbm, down_ref),
-            ]
-        )
+        pltpu.make_async_copy(src, dst, local_sem.at[n]) for n, (src, dst) in enumerate(wanted)
     ]
-    for load in loads:
+    for load in loads[:8]:
         load.start()
 
     def seq_copies(phase, source, target):
@@ -323,14 +340,40 @@
     def rows_of(index):
         return pl.ds(pl.multiple_of(index * TILE, TILE), TILE)
 
+    loads[0].wait()
+    request = lax.broadcasted_iota(jnp.int32, (128, 32), 0) // NEW
+    picked = request == lane_of((128, 32))
+    lens = jnp.sum(
+        jnp.where(picked, lengths_ref[...].astype(f32), 0.0), axis=-1, keepdims=True
+    )
+    lane = lane_of((128, LANES))
+    low = lane < 64
+    token = lax.broadcasted_iota(jnp.int32, (128, LANES), 0)
+    half = HEAD // 2
+    table = np.exp(-np.log(np.float32(ROPE_BASE)) * np.arange(half, dtype=np.float32) / half)
+    lane1 = lane_of((1, LANES)) % half
+    freqs = jnp.zeros((1, LANES), f32)
+    for n in range(half):
+        freqs = jnp.where(lane1 == n, float(table[n]), freqs)
+    angles = (lens + (token % NEW).astype(f32)) * freqs
+    turns = jnp.floor(angles * (1.0 / (2 * np.pi)) + 0.5)
+    angles = ((angles - turns * TURN) - turns * TURN_MIDDLE) - turns * TURN_REST
+    cosine = jnp.cos(angles)
+    sine = jnp.sin(angles)
+    sine = jnp.where(lane % HEAD < half, -sine, sine)
+
+    loads[1].wait()
+    loads[2].wait()
     token_full = tokens_ref[...].astype(f32)
-    normed = rms_scale(token_full, attn_gain_ref[...]).astype(bf16)
-    loads[0].wait()
-    projected = jnp.dot(normed, qkv_ref[...], preferred_element_type=f32)
+    normed = rms_scale(token_full, attn_gain_ref[...].reshape(1, -1)).astype(bf16)
+    projected = jnp.zeros((128, qkv_ref.shape[1]), f32)
+    for n in range(3):
+        at = slice(depth * n, depth * (n + 1))
+        loads[3 + n].wait()
+        projected = projected + jnp.dot(normed[:, at], qkv_ref[at, :], preferred_element_type=f32)
+    for load in loads[8:]:
+        load.start()
     tiles = [projected[:, LANES * n : LANES * (n + 1)] for n in range(5)]
-    lane = lane_of(tiles[0].shape)
-    low = lane < 64
-    cosine, sine = cos_ref[...], sin_ref[...]
 
     def turned(x):
         swapped = jnp.where(lane % 64 < 32, pltpu.roll(x, 96, 1), pltpu.roll(x, 32, 1))
@@ -350,8 +393,27 @@
     new_keys = jnp.where(low, swap_half(turn[1]), swap_half(turn[4])).astype(bf16)
     new_values = jnp.where(low, tiles[2], tiles[4]).astype(bf16)
 
-    loads[1].wait()
-    loads[2].wait()
+    loads[6].wait()
+    loads[7].wait()
+    slot_count = keys_hbm.shape[0] // 32
+    window = float(slot_count * SEQ - SINK)
+    col256 = lane_of((32, 8 * slot_count))
+    row256 = lax.broadcasted_iota(jnp.int32, (32, 8 * slot_count), 0)
+    same = row256 // NEW == col256 // slot_count
+    slot = (me * slot_count + col256 % slot_count).astype(f32)
+    offset = (row256 % NEW).astype(f32)
+    pl.semaphore_wait(barrier, SEQ + TP - 2)
+
+    def send_part(peer):
+        return pltpu.make_async_remote_copy(
+            src_ref=att_send.at[TILE * peer : TILE * (peer + 1), :],
+            dst_ref=att_recv.at[me],
+            send_sem=seq_send.at[0, peer],
+            recv_sem=seq_recv.at[0, me],
+            device_id=(peer, tp),
+            device_id_type=MESH,
+        )
+
     row32 = lax.broadcasted_iota(jnp.int32, (32, 32), 0)
     col32 = lax.broadcasted_iota(jnp.int32, (32, 32), 1)
     own = (row32 // NEW == col32 // NEW) & (col32 <= row32) & (me == 0)
@@ -362,7 +424,12 @@
         at = slice(32 * block, 32 * block + 32)
         slots = slice(256 * block, 256 * block + 256)
         query = jnp.concatenate([q[at] for q in queries], axis=0)
-        old_bias = jnp.concatenate([bias_ref[at, :]] * 6, axis=0)
+        last = lens[at] - 1.0
+        back = last - slot
+        older = last - (back - window * jnp.floor((back + 0.5) * (1.0 / window)))
+        seen = (slot <= last) & ((slot < SINK) | (older > last + offset - window))
+        old_bias = jnp.where(seen & same, 0.0, FLOOR_SCORE).astype(f32)
+        old_bias = jnp.concatenate([old_bias] * 6, axis=0)
         old = lax.dot_general(query, keys_ref[slots, :], contract, preferred_element_type=f32)
         new = lax.dot_general(query, new_keys[at], contract, preferred_element_type=f32)
         old = old + old_bias
@@ -395,28 +462,24 @@
         )
         att_send[at, 384:512] = jnp.where(lane32 < 24, levels, 0.0).astype(bf16)
 
-    pl.semaphore_wait(barrier, SEQ + TP - 2)
-    copies = seq_copies(
-        0, lambda peer: att_send.at[rows_of(peer), :], lambda index: att_recv.at[index]
-    )
+        for peer in (2 * block, 2 * block + 1):
+
+            @pl.when(peer != me)
+            def _(peer=peer):
+                send_part(peer).start()
+
     att_recv[me] = att_send[rows_of(me), :]
 
-    loads[3].wait()
-    loads[4].wait()
-
-    def pack(n, carry):
-        pair_w[n] = jnp.concatenate(
-            [gate_ref[2 * n], up_ref[2 * n], gate_ref[2 * n + 1], up_ref[2 * n + 1]], axis=-1
-        )
-        return carry
-
-    lax.fori_loop(0, EXPERTS // 2, pack, 0)
+    loads[8].wait()
+    routes_ref[...] = jnp.transpose(
+        jnp.concatenate([routes_t_ref[...], jnp.zeros((120, 128), jnp.int32)], axis=0)
+    )
     spread_col = lax.broadcasted_iota(jnp.int32, (TILE, EXPERTS * TILE), 1)
     spread_row = lax.broadcasted_iota(jnp.int32, (TILE, EXPERTS * TILE), 0)
     expert_at = jnp.where(spread_col % TILE == spread_row, spread_col // TILE, -1)
 
     def mark(n, carry):
-        routes = routes_ref[rows_of(n), :]
+        routes = routes_ref[rows_of(n), 0:TOP]
         for k in range(TOP):
             hit = routes[:, k : k + 1] == expert_at
             onehot[n, TILE * k : TILE * (k + 1), :] = jnp.where(hit, 1.0, 0.0).astype(bf16)
@@ -427,8 +490,16 @@
     for k in range(TOP):
         shifted[k] = routes_ref[:, k : k + 1] - half_lane
 
-    for copy in copies:
-        copy.wait()
+    for step in range(1, SEQ):
+        peer = lax.rem(me + step, SEQ)
+        pltpu.make_async_remote_copy(
+            src_ref=att_send.at[rows_of(peer), :],
+            dst_ref=att_recv.at[peer],
+            send_sem=seq_send.at[0, peer],
+            recv_sem=seq_recv.at[0, peer],
+            device_id=(peer, tp),
+            device_id_type=MESH,
+        ).wait()
     own_level = []
     for n in range(SEQ):
         packed = att_recv[n, :, 384:512].astype(f32)
@@ -453,7 +524,7 @@
         tp_copy(step, att_all.at[tp], att_all.at[tp], lax.rem(tp + step, TP))
         for step in range(1, TP)
     ]
-    loads[5].wait()
+    loads[11].wait()
     width = out_w_ref.shape[1]
     residual = tokens_ref[rows_of(me), pl.ds(pl.multiple_of(tp * width, 128), width)].astype(f32)
     for copy in copies:
@@ -469,13 +540,15 @@
         copy.wait()
 
     full = res_all[...].reshape(SEQ * TILE, width).astype(f32)
-    gained = full * moe_gain_ref[...]
+    loads[9].wait()
+    loads[10].wait()
+    gained = full * moe_gain_ref[...].reshape(1, -1)
     gained_b = gained.astype(bf16)
     rest = (gained - gained_b.astype(f32)).astype(bf16)
     router = router_ref[...]
-    logits = jnp.dot(gained_b, router, preferred_element_type=f32) + jnp.dot(
-        rest, router, preferred_element_type=f32
-    )
+    logits = lax.dot_general(
+        gained_b, router, contract, preferred_element_type=f32
+    ) + lax.dot_general(rest, router, contract, preferred_element_type=f32)
     squares = jnp.sum(full * full, axis=-1, keepdims=True)
     logit_rows[...] = jnp.zeros_like(logit_rows)
     logit_rows[:, 0:EXPERTS] = logits
@@ -483,8 +556,14 @@
     rows = split_pair(jnp.where(low, rows, swap_half(rows)))
     picks[:, TOP * TILE :, :] = rows.reshape(8, TILE, LANES)
 
+    loads[12].wait()
+    loads[13].wait()
+
     def experts(n, carry):
-        both = jnp.dot(gained_b, pair_w[n], preferred_element_type=f32).astype(bf16)
+        weight = pair_w[pl.ds(2 * n, 2)].reshape(2 * LANES, width)
+        both = lax.dot_general(
+            gained_b, weight, contract, preferred_element_type=f32
+        ).astype(bf16)
         dense[2 * n] = both[:, :LANES]
         dense[2 * n + 1] = both[:, LANES:]
         return carry
@@ -498,49 +577,69 @@
         ).astype(bf16)
         return carry
 
-    lax.fori_loop(0, 8, pick, 0)
-
-    mine = pl.ds(4 * core, 4)
-    copy = tp_copy(4, picks.at[pl.ds(4 * (1 - core), 4)], picks_recv, core_peer)
-    copy.wait()
-    picks_half[:, 0 : TOP * TILE, :] = (
-        picks[mine, 0 : TOP * TILE, :].astype(f32) + picks_recv[:, 0 : TOP * TILE, :].astype(f32)
-    ).astype(bf16)
-    ours = picks[mine, TOP * TILE :, :].reshape(64, LANES)
-    theirs = picks_recv[:, TOP * TILE :, :].reshape(64, LANES)
-    picks_half[:, TOP * TILE :, :] = split_pair(join_pair(ours) + join_pair(theirs)).reshape(
-        4, TILE, LANES
-    )
-    copy = tp_copy(5, picks_half, picks_far, far_peer)
-    copy.wait()
-    rows = join_pair(picks_half[:, TOP * TILE :, :].reshape(64, LANES)) + join_pair(
-        picks_far[:, TOP * TILE :, :].reshape(64, LANES)
-    )
-    lane64 = lane_of((64, LANES))
-    low64 = lane64 < 64
-    scale = lax.rsqrt(rows[:, EXPERTS : EXPERTS + 1] / D + EPSILON)
-    routes = routes_ref[pl.ds(pl.multiple_of(64 * core, 64), 64), :]
-    hits = [lane64 == routes[:, k : k + 1] for k in range(TOP)]
-    routed = hits[0]
-    for k in range(1, TOP):
-        routed = routed | hits[k]
-    scores = jnp.where(routed, rows * scale, FLOOR_SCORE)
-    prob = jnp.exp(scores - jnp.max(scores, axis=-1, keepdims=True))
-    prob = jnp.where(routed, prob, 0.0)
-    prob = prob / jnp.sum(prob, axis=-1, keepdims=True)
-    for k in range(TOP):
-        at = slice(TILE * k, TILE * (k + 1))
-        both = (picks_half[:, at, :].astype(f32) + picks_far[:, at, :].astype(f32)).reshape(
-            64, LANES
-        ) * scale
-        active = both / (1.0 + jnp.exp(-both)) * swap_half(both)
-        active = active.astype(bf16).astype(f32)
-        active = active * jnp.sum(jnp.where(hits[k], prob, 0.0), axis=-1, keepdims=True)
-        active = jnp.where(low64, active, swap_half(active))
-        scaled[mine, at, :] = active.astype(bf16).reshape(4, TILE, LANES)
-    copy = tp_copy(6, scaled.at[mine], scaled.at[mine], core_peer)
-    loads[6].wait()
-    copy.wait()
+    groups = 4 // CHUNKS
+    count = groups * TILE
+    near, far, back = [], [], []
+    for chunk in range(CHUNKS):
+        first = 4 * (1 - core) + groups * chunk
+        lax.fori_loop(first, first + groups, pick, 0)
+        at = slice(groups * chunk, groups * (chunk + 1))
+        near.append(
+            tp_copy(4 + chunk, picks.at[pl.ds(first, groups)], picks_recv.at[at], core_peer)
+        )
+    lax.fori_loop(4 * core, 4 * core + 4, pick, 0)
+    for chunk in range(CHUNKS):
+        at = slice(groups * chunk, groups * (chunk + 1))
+        mine = pl.ds(4 * core + groups * chunk, groups)
+        near[chunk].wait()
+        picks_half[at, 0 : TOP * TILE, :] = (
+            picks[mine, 0 : TOP * TILE, :].astype(f32)
+            + picks_recv[at, 0 : TOP * TILE, :].astype(f32)
+        ).astype(bf16)
+        ours = picks[mine, TOP * TILE :, :].reshape(count, LANES)
+        theirs = picks_recv[at, TOP * TILE :, :].reshape(count, LANES)
+        picks_half[at, TOP * TILE :, :] = split_pair(join_pair(ours) + join_pair(theirs)).reshape(
+            groups, TILE, LANES
+        )
+        far.append(
+            tp_copy(4 + CHUNKS + chunk, picks_half.at[at], picks_far.at[at], far_peer)
+        )
+    lanes = lane_of((count, LANES))
+    low_part = lanes < 64
+    for chunk in range(CHUNKS):
+        at = slice(groups * chunk, groups * (chunk + 1))
+        mine = pl.ds(4 * core + groups * chunk, groups)
+        far[chunk].wait()
+        rows = join_pair(picks_half[at, TOP * TILE :, :].reshape(count, LANES)) + join_pair(
+            picks_far[at, TOP * TILE :, :].reshape(count, LANES)
+        )
+        scale = lax.rsqrt(rows[:, EXPERTS : EXPERTS + 1] / D + EPSILON)
+        start = pl.multiple_of(64 * core + count * chunk, count)
+        routes = routes_ref[pl.ds(start, count), 0:TOP]
+        hits = [lanes == routes[:, k : k + 1] for k in range(TOP)]
+        routed = hits[0]
+        for k in range(1, TOP):
+            routed = routed | hits[k]
+        scores = jnp.where(routed, rows * scale, FLOOR_SCORE)
+        prob = jnp.exp(scores - jnp.max(scores, axis=-1, keepdims=True))
+        prob = jnp.where(routed, prob, 0.0)
+        prob = prob / jnp.sum(prob, axis=-1, keepdims=True)
+        for k in range(TOP):
+            of = slice(TILE * k, TILE * (k + 1))
+            both = (picks_half[at, of, :].astype(f32) + picks_far[at, of, :].astype(f32)).reshape(
+                count, LANES
+            ) * scale
+            active = both / (1.0 + jnp.exp(-both)) * swap_half(both)
+            active = active.astype(bf16).astype(f32)
+            active = active * jnp.sum(jnp.where(hits[k], prob, 0.0), axis=-1, keepdims=True)
+            active = jnp.where(low_part, active, swap_half(active))
+            scaled[mine, of, :] = active.astype(bf16).reshape(groups, TILE, LANES)
+        back.append(
+            tp_copy(4 + 2 * CHUNKS + chunk, scaled.at[mine], scaled.at[mine], core_peer)
+        )
+    loads[14].wait()
+    for copy in back:
+        copy.wait()
 
     for k in range(TOP):
         scaled_f[k] = scaled[:, TILE * k : TILE * (k + 1), :].reshape(128, LANES).astype(f32)
@@ -593,54 +692,37 @@
     lengths,
     routes,
 ):
-    seq_index = lax.axis_index("seq")
     count = tokens.shape[0]
     width = out_weight.shape[1]
     requests, slot_count = cache_keys.shape[:2]
-    window = slot_count * SEQ - SINK
-    places = (
-        (lengths[:, None] + jnp.arange(NEW, dtype=jnp.int32)[None, :])
-        .reshape(count)
-        .astype(jnp.float32)
-    )
-    lane = jnp.arange(LANES, dtype=jnp.int32)
-    half = HEAD // 2
-    freqs = jnp.exp(-jnp.log(ROPE_BASE) * (lane % half).astype(jnp.float32) / half)
-    angles = places[:, None] * freqs[None, :]
-    cosine = jnp.cos(angles)
-    sine = jnp.where((lane % HEAD < half)[None, :], -jnp.sin(angles), jnp.sin(angles))
-    column = jnp.arange(8 * slot_count, dtype=jnp.int32)
-    token = jnp.arange(count, dtype=jnp.int32)
-    lens = jnp.repeat(lengths, NEW)[:, None]
-    slot = (seq_index * slot_count + column % slot_count)[None, :]
-    older = lens - 1 - jnp.mod(lens - 1 - slot, window)
-    seen = (slot < lens) & ((slot < SINK) | (older >= lens + (token % NEW)[:, None] - window))
-    same = ((token // NEW) % 8)[:, None] == (column // slot_count)[None, :]
-    bias = jnp.where(seen & same, 0.0, FLOOR_SCORE).astype(jnp.float32)
-
     vmem = pl.BlockSpec(memory_space=pltpu.VMEM)
-    anywhere = pl.BlockSpec(memory_space=pl.ANY)
+    hbm = pl.BlockSpec(memory_space=pltpu.HBM)
     bf16, f32 = jnp.bfloat16, jnp.float32
     hidden = expert_gate.shape[2]
     return pl.pallas_call(
         layer_kernel,
         out_shape=jax.ShapeDtypeStruct((count, width), bf16),
-        in_specs=[vmem] * 8 + [anywhere] * 7,
+        in_specs=[hbm] * 13,
         out_specs=vmem,
         scratch_shapes=[
+            pltpu.VMEM(tokens.shape, bf16),
+            pltpu.VMEM((D,), f32),
+            pltpu.VMEM((width,), f32),
+            pltpu.VMEM((1, requests), jnp.int32),
+            pltpu.VMEM((TOP, count), jnp.int32),
+            pltpu.VMEM((EXPERTS, width), bf16),
+            pltpu.VMEM((count, count), jnp.int32),
             pltpu.VMEM(qkv_weight.shape, bf16),
             pltpu.VMEM((requests * slot_count, LANES), bf16),
             pltpu.VMEM((requests * slot_count, LANES), bf16),
             pltpu.VMEM(out_weight.shape, bf16),
-            pltpu.VMEM(expert_gate.shape, bf16),
-            pltpu.VMEM(expert_up.shape, bf16),
             pltpu.VMEM(expert_down.shape, bf16),
             pltpu.VMEM((count, 512), bf16),
             pltpu.VMEM((SEQ, TILE, 512), bf16),
             pltpu.VMEM((TP, TILE, width), bf16),
             pltpu.VMEM((TILE, width), f32),
             pltpu.VMEM((SEQ, TILE, width), bf16),
-            pltpu.VMEM((EXPERTS // 2, width, 4 * hidden), bf16),
+            pltpu.VMEM((EXPERTS, 2 * hidden, width), bf16),
             pltpu.VMEM((EXPERTS, count, LANES), bf16),
             pltpu.VMEM((8, TOP * TILE, EXPERTS * TILE), bf16),
             pltpu.VMEM((TOP, count, LANES), jnp.int32),
@@ -655,14 +737,14 @@
             pltpu.VMEM((count, width), bf16),
             pltpu.VMEM((SEQ, TILE, width), bf16),
             pltpu.VMEM((TILE, width), bf16),
-            pltpu.SemaphoreType.DMA((7,)),
+            pltpu.SemaphoreType.DMA((15,)),
             pltpu.SemaphoreType.DMA((4, SEQ)),
             pltpu.SemaphoreType.DMA((4, SEQ)),
-            pltpu.SemaphoreType.DMA((7,)),
-            pltpu.SemaphoreType.DMA((7,)),
+            pltpu.SemaphoreType.DMA((4 + 3 * CHUNKS,)),
+            pltpu.SemaphoreType.DMA((4 + 3 * CHUNKS,)),
         ],
         compiler_params=pltpu.CompilerParams(
-            collective_id=0, has_side_effects=True, vmem_limit_bytes=48 * 1024 * 1024
+            collective_id=0, has_side_effects=True, vmem_limit_bytes=VMEM_LIMIT
         ),
         cost_estimate=pl.CostEstimate(
             flops=2_000_000_000, bytes_accessed=20_000_000, transcendentals=1_000_000
@@ -670,19 +752,17 @@
         name="layer",
     )(
         tokens,
-        attn_gain.reshape(1, -1),
-        moe_gain.reshape(1, -1),
-        cosine,
-        sine,
-        bias,
-        routes,
-        router_weight,
+        attn_gain,
+        moe_gain,
+        lengths.reshape(1, -1),
+        routes.T,
+        router_weight.T,
         qkv_weight,
         cache_keys.reshape(-1, LANES),
         cache_values.reshape(-1, LANES),
         out_weight,
-        expert_gate,
-        expert_up,
+        jnp.swapaxes(expert_gate, 1, 2),
+        jnp.swapaxes(expert_up, 1, 2),
         expert_down,
     )
 

time: 64.4 us -> 47.5 us (0.74)
  local copies, waits for them, and re-layouts: 17.9 us -> 1.54 us
  other arithmetic: 1.18 us -> 0 us
  Pallas kernels: 44.7 us -> 45.8 us
    unnamed x17 -> x1, local copies, waits for them, and re-layouts: 15.6 us -> 1.54 us
    reshape x2 -> x0, local copies, waits for them, and re-layouts: 1.39 us -> none  [the longest x1 0.7 us: fused_device(): attn_gain.reshape(1, -1)]
    select_n x3 -> x0, other arithmetic: 1.16 us -> none  [the longest x1 0.95 us: fused_device(): jnp.where((lane % HEAD < half)[None, :], -jnp.sin(angles), jnp.sin(angles))]
    pallas_call x1, Pallas kernels: 44.7 us -> 45.8 us  [fused_device(): pl.pallas_call(layer_kernel, out_shape=jax.ShapeDtypeStruct((count, width...]
    add x4 -> x0, local copies, waits for them, and re-layouts: 0.93 us -> none  [fused_device(): lengths[:, None] + jnp.arange(NEW, dtype=jnp.int32)[None, :]]
where the time goes in v2:
time: 47.5 us; the launch traced here: 47.3 us
  Pallas kernels  45.8 us (96%)
  local copies, waits for them, and re-layouts  1.54 us (3%)
    pallas_call x1, Pallas kernels, fused_device(): pl.pallas_call(layer_kernel, out_shape=jax.ShapeDtypeStruct((count, width...  45.8 us
    unnamed x1, local copies, waits for them, and re-layouts  1.54 us

profile of v2, /device:TPU:0, one launch (start us, length us, event | category | flops | bytes accessed | tf_op | source)
XLA Modules:
  0.0 47.3 jit_solution(6020762758184796506)
XLA Ops:
  0.0 45.8 %layer.1 = bf16[128,384]{1,0:T(8,128)(2,1)} custom-call(bf16[128,1536]{1,0:T(8,128)(2,1)} %tokens_hbm.1, f32[1536]{0:T(1024)} %attn_gain_hbm.1, f32[384]{0:T(512)} %moe_gain_hbm.1, s32[1,32]{1,0:T(1,128)} %bitcast.13, s32[8,128]{1,0:T(8,128)} %bitcast.12, bf16[40,384]{1,0:T(8,128)(2,1)} %bitcast.11, bf16[1536,640]{1,0:T(8,128)(2,1)} %qkv_hbm.1, ...), custom_call_target="tpu_custom_call" | custom-call | flops 2000000000 | bytes 20000000 | tf_op jit(solution)/shard_map/layer/pallas_call | solution.py:702
  45.8 1.5 %copy.15 = bf16[128,384]{1,0:T(8,128)(2,1)} copy(bf16[128,384]{1,0:T(8,128)(2,1)} %layer.1) | data formatting | bytes 196608

commit v3 on v2

--- a/solution.py
+++ b/solution.py
@@ -184,7 +184,7 @@
 TP = 4
 MESH = pl.DeviceIdType.MESH
 CHUNKS = 2
-VMEM_LIMIT = 62 * 1024 * 1024
+VMEM_LIMIT = 61 * 1024 * 1024
 TURN = 6.28125
 TURN_MIDDLE = 0.0019350051879882812
 TURN_REST = 3.0199159819568123e-07
@@ -485,7 +485,7 @@
             onehot[n, TILE * k : TILE * (k + 1), :] = jnp.where(hit, 1.0, 0.0).astype(bf16)
         return carry
 
-    lax.fori_loop(0, 8, mark, 0)
+    lax.fori_loop(0, 8, mark, 0, unroll=2)
     half_lane = jnp.where(low, 0, 1)
     for k in range(TOP):
         shifted[k] = routes_ref[:, k : k + 1] - half_lane
@@ -568,7 +568,7 @@
         dense[2 * n + 1] = both[:, LANES:]
         return carry
 
-    lax.fori_loop(0, EXPERTS // 2, experts, 0)
+    lax.fori_loop(0, EXPERTS // 2, experts, 0, unroll=5)
 
     def pick(n, carry):
         group = dense[:, rows_of(n), :].reshape(EXPERTS * TILE, LANES)
@@ -582,12 +582,14 @@
     near, far, back = [], [], []
     for chunk in range(CHUNKS):
         first = 4 * (1 - core) + groups * chunk
-        lax.fori_loop(first, first + groups, pick, 0)
+        for n in range(groups):
+            pick(first + n, 0)
         at = slice(groups * chunk, groups * (chunk + 1))
         near.append(
             tp_copy(4 + chunk, picks.at[pl.ds(first, groups)], picks_recv.at[at], core_peer)
         )
-    lax.fori_loop(4 * core, 4 * core + 4, pick, 0)
+    for n in range(4):
+        pick(4 * core + n, 0)
     for chunk in range(CHUNKS):
         at = slice(groups * chunk, groups * (chunk + 1))
         mine = pl.ds(4 * core + groups * chunk, groups)
@@ -658,7 +660,7 @@
         total[...] += jnp.dot(spread, weight, preferred_element_type=f32)
         return carry
 
-    lax.fori_loop(0, EXPERTS // 4, down, 0)
+    lax.fori_loop(0, EXPERTS // 4, down, 0, unroll=5)
     part_send[...] = total[...].astype(bf16)
 
     copies = seq_copies(
@@ -701,7 +703,7 @@
     hidden = expert_gate.shape[2]
     return pl.pallas_call(
         layer_kernel,
-        out_shape=jax.ShapeDtypeStruct((count, width), bf16),
+        out_shape=pltpu.VMEM((count, width), bf16),
         in_specs=[hbm] * 13,
         out_specs=vmem,
         scratch_shapes=[

time: 47.5 us -> 42.2 us (0.89)
  Pallas kernels: 45.8 us -> 41.4 us
  local copies, waits for them, and re-layouts: 1.54 us -> 0.64 us
    pallas_call x1, Pallas kernels: 45.8 us -> 41.4 us  [fused_device(): pl.pallas_call(layer_kernel, out_shape=pltpu.VMEM((count, width), bf16),...]
    unnamed x1, local copies, waits for them, and re-layouts: 1.54 us -> 0.64 us
where the time goes in v3:
time: 42.2 us; the launch traced here: 42 us
  Pallas kernels  41.4 us (98%)
  local copies, waits for them, and re-layouts  0.64 us (2%)
    pallas_call x1, Pallas kernels, fused_device(): pl.pallas_call(layer_kernel, out_shape=pltpu.VMEM((count, width), bf16),...  41.4 us

profile of v3, /device:TPU:0, one launch (start us, length us, event | category | flops | bytes accessed | tf_op | source)
XLA Modules:
  0.0 42.0 jit_solution(6292381782781405586)
XLA Ops:
  0.0 41.4 %layer.1 = bf16[128,384]{1,0:T(8,128)(2,1)S(1)} custom-call(bf16[128,1536]{1,0:T(8,128)(2,1)} %tokens_hbm.1, f32[1536]{0:T(1024)} %attn_gain_hbm.1, f32[384]{0:T(512)} %moe_gain_hbm.1, s32[1,32]{1,0:T(1,128)} %bitcast.13, s32[8,128]{1,0:T(8,128)} %bitcast.12, bf16[40,384]{1,0:T(8,128)(2,1)} %bitcast.11, bf16[1536,640]{1,0:T(8,128)(2,1)} %qkv_hbm.1, ...), custom_call_target="tpu_custom_call" | custom-call | flops 2000000000 | bytes 20000000 | tf_op jit(solution)/shard_map/layer/pallas_call | solution.py:704
  41.4 0.6 %copy.15 = bf16[128,384]{1,0:T(8,128)(2,1)} copy(bf16[128,384]{1,0:T(8,128)(2,1)S(1)} %layer.1) | data formatting | bytes 196608

commit v4 on v3

--- a/solution.py
+++ b/solution.py
@@ -210,6 +210,19 @@
 def join_pair(packed):
     values = packed.astype(jnp.float32)
     return values + swap_half(values)
+
+
+def circle(angles):
+    half = angles * 0.5
+    square = half * half
+    sine = jnp.full_like(square, 1.0 / 6227020800.0)
+    cosine = jnp.full_like(square, -1.0 / 87178291200.0)
+    for term in (-39916800.0, 362880.0, -5040.0, 120.0, -6.0, 1.0):
+        sine = sine * square + 1.0 / term
+    for term in (479001600.0, -3628800.0, 40320.0, -720.0, 24.0, -2.0, 1.0):
+        cosine = cosine * square + 1.0 / term
+    sine = sine * half
+    return 1.0 - 2.0 * sine * sine, 2.0 * sine * cosine
 
 
 def layer_kernel(
@@ -253,8 +266,13 @@
     picks_half,
     picks_far,
     logit_rows,
+    sums,
+    sums_recv,
+    sums_half,
+    sums_far,
+    gate_scale,
     scaled,
-    scaled_f,
+    spread,
     total,
     part_send,
     part_recv,
@@ -358,8 +376,7 @@
     angles = (lens + (token % NEW).astype(f32)) * freqs
     turns = jnp.floor(angles * (1.0 / (2 * np.pi)) + 0.5)
     angles = ((angles - turns * TURN) - turns * TURN_MIDDLE) - turns * TURN_REST
-    cosine = jnp.cos(angles)
-    sine = jnp.sin(angles)
+    cosine, sine = circle(angles)
     sine = jnp.where(lane % HEAD < half, -sine, sine)
 
     loads[1].wait()
@@ -402,18 +419,6 @@
     same = row256 // NEW == col256 // slot_count
     slot = (me * slot_count + col256 % slot_count).astype(f32)
     offset = (row256 % NEW).astype(f32)
-    pl.semaphore_wait(barrier, SEQ + TP - 2)
-
-    def send_part(peer):
-        return pltpu.make_async_remote_copy(
-            src_ref=att_send.at[TILE * peer : TILE * (peer + 1), :],
-            dst_ref=att_recv.at[me],
-            send_sem=seq_send.at[0, peer],
-            recv_sem=seq_recv.at[0, me],
-            device_id=(peer, tp),
-            device_id_type=MESH,
-        )
-
     row32 = lax.broadcasted_iota(jnp.int32, (32, 32), 0)
     col32 = lax.broadcasted_iota(jnp.int32, (32, 32), 1)
     own = (row32 // NEW == col32 // NEW) & (col32 <= row32) & (me == 0)
@@ -462,12 +467,10 @@
         )
         att_send[at, 384:512] = jnp.where(lane32 < 24, levels, 0.0).astype(bf16)
 
-        for peer in (2 * block, 2 * block + 1):
-
-            @pl.when(peer != me)
-            def _(peer=peer):
-                send_part(peer).start()
-
+    pl.semaphore_wait(barrier, SEQ + TP - 2)
+    copies = seq_copies(
+        0, lambda peer: att_send.at[rows_of(peer), :], lambda index: att_recv.at[index]
+    )
     att_recv[me] = att_send[rows_of(me), :]
 
     loads[8].wait()
@@ -490,16 +493,8 @@
     for k in range(TOP):
         shifted[k] = routes_ref[:, k : k + 1] - half_lane
 
-    for step in range(1, SEQ):
-        peer = lax.rem(me + step, SEQ)
-        pltpu.make_async_remote_copy(
-            src_ref=att_send.at[rows_of(peer), :],
-            dst_ref=att_recv.at[peer],
-            send_sem=seq_send.at[0, peer],
-            recv_sem=seq_recv.at[0, peer],
-            device_id=(peer, tp),
-            device_id_type=MESH,
-        ).wait()
+    for copy in copies:
+        copy.wait()
     own_level = []
     for n in range(SEQ):
         packed = att_recv[n, :, 384:512].astype(f32)
@@ -554,7 +549,13 @@
     logit_rows[:, 0:EXPERTS] = logits
     rows = jnp.where(lane == EXPERTS, squares, logit_rows[...])
     rows = split_pair(jnp.where(low, rows, swap_half(rows)))
-    picks[:, TOP * TILE :, :] = rows.reshape(8, TILE, LANES)
+    sums[...] = rows
+    sums_copy = tp_copy(
+        4 + 3 * CHUNKS,
+        sums.at[pl.ds(pl.multiple_of(64 * (1 - core), 64), 64), :],
+        sums_recv,
+        core_peer,
+    )
 
     loads[12].wait()
     loads[13].wait()
@@ -568,7 +569,7 @@
         dense[2 * n + 1] = both[:, LANES:]
         return carry
 
-    lax.fori_loop(0, EXPERTS // 2, experts, 0, unroll=5)
+    lax.fori_loop(0, EXPERTS // 2, experts, 0, unroll=10)
 
     def pick(n, carry):
         group = dense[:, rows_of(n), :].reshape(EXPERTS * TILE, LANES)
@@ -590,77 +591,77 @@
         )
     for n in range(4):
         pick(4 * core + n, 0)
+    sums_copy.wait()
+    ours = pl.ds(pl.multiple_of(64 * core, 64), 64)
+    sums_half[...] = split_pair(join_pair(sums[ours, :]) + join_pair(sums_recv[...]))
+    sums_copy = tp_copy(5 + 3 * CHUNKS, sums_half, sums_far, far_peer)
     for chunk in range(CHUNKS):
         at = slice(groups * chunk, groups * (chunk + 1))
         mine = pl.ds(4 * core + groups * chunk, groups)
         near[chunk].wait()
-        picks_half[at, 0 : TOP * TILE, :] = (
-            picks[mine, 0 : TOP * TILE, :].astype(f32)
-            + picks_recv[at, 0 : TOP * TILE, :].astype(f32)
-        ).astype(bf16)
-        ours = picks[mine, TOP * TILE :, :].reshape(count, LANES)
-        theirs = picks_recv[at, TOP * TILE :, :].reshape(count, LANES)
-        picks_half[at, TOP * TILE :, :] = split_pair(join_pair(ours) + join_pair(theirs)).reshape(
-            groups, TILE, LANES
-        )
+        picks_half[at] = (picks[mine].astype(f32) + picks_recv[at].astype(f32)).astype(bf16)
         far.append(
             tp_copy(4 + CHUNKS + chunk, picks_half.at[at], picks_far.at[at], far_peer)
         )
-    lanes = lane_of((count, LANES))
-    low_part = lanes < 64
+
+    sums_copy.wait()
+    rows = join_pair(sums_half[...]) + join_pair(sums_far[...])
+    lanes = lane_of((64, LANES))
+    scales = lax.rsqrt(rows[:, EXPERTS : EXPERTS + 1] / D + EPSILON)
+    routes = routes_ref[ours, 0:TOP]
+    hits = [lanes == routes[:, k : k + 1] for k in range(TOP)]
+    routed = hits[0]
+    for k in range(1, TOP):
+        routed = routed | hits[k]
+    scores = jnp.where(routed, rows * scales, FLOOR_SCORE)
+    prob = jnp.exp(scores - jnp.max(scores, axis=-1, keepdims=True))
+    prob = jnp.where(routed, prob, 0.0)
+    prob = prob / jnp.sum(prob, axis=-1, keepdims=True)
+    probs = [jnp.sum(jnp.where(hits[k], prob, 0.0), axis=-1, keepdims=True) for k in range(TOP)]
+    for k in range(TOP):
+        gate_scale[k] = jnp.broadcast_to(probs[k], (64, LANES))
+    gate_scale[TOP] = jnp.broadcast_to(scales, (64, LANES))
+    low_part = lane_of((count, LANES)) < 64
     for chunk in range(CHUNKS):
         at = slice(groups * chunk, groups * (chunk + 1))
         mine = pl.ds(4 * core + groups * chunk, groups)
+        part = slice(count * chunk, count * (chunk + 1))
         far[chunk].wait()
-        rows = join_pair(picks_half[at, TOP * TILE :, :].reshape(count, LANES)) + join_pair(
-            picks_far[at, TOP * TILE :, :].reshape(count, LANES)
-        )
-        scale = lax.rsqrt(rows[:, EXPERTS : EXPERTS + 1] / D + EPSILON)
-        start = pl.multiple_of(64 * core + count * chunk, count)
-        routes = routes_ref[pl.ds(start, count), 0:TOP]
-        hits = [lanes == routes[:, k : k + 1] for k in range(TOP)]
-        routed = hits[0]
-        for k in range(1, TOP):
-            routed = routed | hits[k]
-        scores = jnp.where(routed, rows * scale, FLOOR_SCORE)
-        prob = jnp.exp(scores - jnp.max(scores, axis=-1, keepdims=True))
-        prob = jnp.where(routed, prob, 0.0)
-        prob = prob / jnp.sum(prob, axis=-1, keepdims=True)
+        scale = gate_scale[TOP, part, :]
         for k in range(TOP):
             of = slice(TILE * k, TILE * (k + 1))
             both = (picks_half[at, of, :].astype(f32) + picks_far[at, of, :].astype(f32)).reshape(
                 count, LANES
             ) * scale
             active = both / (1.0 + jnp.exp(-both)) * swap_half(both)
-            active = active.astype(bf16).astype(f32)
-            active = active * jnp.sum(jnp.where(hits[k], prob, 0.0), axis=-1, keepdims=True)
+            active = active.astype(bf16).astype(f32) * gate_scale[k, part, :]
             active = jnp.where(low_part, active, swap_half(active))
             scaled[mine, of, :] = active.astype(bf16).reshape(groups, TILE, LANES)
         back.append(
             tp_copy(4 + 2 * CHUNKS + chunk, scaled.at[mine], scaled.at[mine], core_peer)
         )
+
+    def spread_rows(n):
+        values = [
+            scaled[n, TILE * k : TILE * (k + 1), :].astype(f32) for k in range(TOP)
+        ]
+        routes = [shifted[k, rows_of(n), :] for k in range(TOP)]
+        for pair in range(EXPERTS // 2):
+            one = jnp.zeros((TILE, LANES), f32)
+            for k in range(TOP):
+                one = jnp.where(routes[k] == 2 * pair, values[k], one)
+            spread[rows_of(n), LANES * pair : LANES * (pair + 1)] = one.astype(bf16)
+
+    for n in range(4):
+        spread_rows(4 * core + n)
     loads[14].wait()
-    for copy in back:
-        copy.wait()
-
-    for k in range(TOP):
-        scaled_f[k] = scaled[:, TILE * k : TILE * (k + 1), :].reshape(128, LANES).astype(f32)
-    total[...] = jnp.zeros_like(total)
-
-    def down(n, carry):
-        spread = []
-        for pair in range(2):
-            wanted = 4 * n + 2 * pair
-            one = jnp.zeros((128, LANES), f32)
-            for k in range(TOP):
-                one = jnp.where(shifted[k] == wanted, scaled_f[k], one)
-            spread.append(one)
-        spread = jnp.concatenate(spread, axis=-1).astype(bf16)
-        weight = down_ref[pl.ds(4 * n, 4)].reshape(256, width)
-        total[...] += jnp.dot(spread, weight, preferred_element_type=f32)
-        return carry
-
-    lax.fori_loop(0, EXPERTS // 4, down, 0, unroll=5)
+    for chunk in range(CHUNKS):
+        back[chunk].wait()
+        for n in range(groups):
+            spread_rows(4 * (1 - core) + groups * chunk + n)
+    total[...] = jnp.dot(
+        spread[...], down_ref[...].reshape(EXPERTS * hidden, width), preferred_element_type=f32
+    )
     part_send[...] = total[...].astype(bf16)
 
     copies = seq_copies(
@@ -728,13 +729,18 @@
             pltpu.VMEM((EXPERTS, count, LANES), bf16),
             pltpu.VMEM((8, TOP * TILE, EXPERTS * TILE), bf16),
             pltpu.VMEM((TOP, count, LANES), jnp.int32),
-            pltpu.VMEM((8, (TOP + 1) * TILE, LANES), bf16),
-            pltpu.VMEM((4, (TOP + 1) * TILE, LANES), bf16),
-            pltpu.VMEM((4, (TOP + 1) * TILE, LANES), bf16),
-            pltpu.VMEM((4, (TOP + 1) * TILE, LANES), bf16),
+            pltpu.VMEM((8, TOP * TILE, LANES), bf16),
+            pltpu.VMEM((4, TOP * TILE, LANES), bf16),
+            pltpu.VMEM((4, TOP * TILE, LANES), bf16),
+            pltpu.VMEM((4, TOP * TILE, LANES), bf16),
             pltpu.VMEM((count, LANES), f32),
+            pltpu.VMEM((count, LANES), bf16),
+            pltpu.VMEM((64, LANES), bf16),
+            pltpu.VMEM((64, LANES), bf16),
+            pltpu.VMEM((64, LANES), bf16),
+            pltpu.VMEM((TOP + 1, 64, LANES), f32),
             pltpu.VMEM((8, TOP * TILE, LANES), bf16),
-            pltpu.VMEM((TOP, count, LANES), f32),
+            pltpu.VMEM((count, EXPERTS * hidden), bf16),
             pltpu.VMEM((count, width), f32),
             pltpu.VMEM((count, width), bf16),
             pltpu.VMEM((SEQ, TILE, width), bf16),
@@ -742,8 +748,8 @@
             pltpu.SemaphoreType.DMA((15,)),
             pltpu.SemaphoreType.DMA((4, SEQ)),
             pltpu.SemaphoreType.DMA((4, SEQ)),
-            pltpu.SemaphoreType.DMA((4 + 3 * CHUNKS,)),
-            pltpu.SemaphoreType.DMA((4 + 3 * CHUNKS,)),
+            pltpu.SemaphoreType.DMA((6 + 3 * CHUNKS,)),
+            pltpu.SemaphoreType.DMA((6 + 3 * CHUNKS,)),
         ],
         compiler_params=pltpu.CompilerParams(
             collective_id=0, has_side_effects=True, vmem_limit_bytes=VMEM_LIMIT

time: 42.2 us -> 39.9 us (0.945)
  Pallas kernels: 41.4 us -> 39.1 us
    pallas_call x1, Pallas kernels: 41.4 us -> 39.1 us  [fused_device(): pl.pallas_call(layer_kernel, out_shape=pltpu.VMEM((count, width), bf16),...]
where the time goes in v4:
time: 39.9 us; the launch traced here: 39.8 us
  Pallas kernels  39.1 us (98%)
  local copies, waits for them, and re-layouts  0.64 us (2%)
    pallas_call x1, Pallas kernels, fused_device(): pl.pallas_call(layer_kernel, out_shape=pltpu.VMEM((count, width), bf16),...  39.1 us

profile of v4, /device:TPU:0, one launch (start us, length us, event | category | flops | bytes accessed | tf_op | source)
XLA Modules:
  0.0 39.8 jit_solution(3443349762249823452)
XLA Ops:
  0.0 39.1 %layer.1 = bf16[128,384]{1,0:T(8,128)(2,1)S(1)} custom-call(bf16[128,1536]{1,0:T(8,128)(2,1)} %tokens_hbm.1, f32[1536]{0:T(1024)} %attn_gain_hbm.1, f32[384]{0:T(512)} %moe_gain_hbm.1, s32[1,32]{1,0:T(1,128)} %bitcast.13, s32[8,128]{1,0:T(8,128)} %bitcast.12, bf16[40,384]{1,0:T(8,128)(2,1)} %bitcast.11, bf16[1536,640]{1,0:T(8,128)(2,1)} %qkv_hbm.1, ...), custom_call_target="tpu_custom_call" | custom-call | flops 2000000000 | bytes 20000000 | tf_op jit(solution)/shard_map/layer/pallas_call | solution.py:705
  39.1 0.6 %copy.15 = bf16[128,384]{1,0:T(8,128)(2,1)} copy(bf16[128,384]{1,0:T(8,128)(2,1)S(1)} %layer.1) | data formatting | bytes 196608

commit v5 on v4

--- a/solution.py
+++ b/solution.py
@@ -271,6 +271,10 @@
     sums_half,
     sums_far,
     gate_scale,
+    queries_ref,
+    new_keys_ref,
+    new_values_ref,
+    lens_ref,
     scaled,
     spread,
     total,
@@ -406,9 +410,11 @@
         jnp.where(low, 0.0, swap_half(turn[3])),
         jnp.where(low, 0.0, turn[3]),
     ]
-    queries = [(q * factor).astype(bf16) for q in queries]
-    new_keys = jnp.where(low, swap_half(turn[1]), swap_half(turn[4])).astype(bf16)
-    new_values = jnp.where(low, tiles[2], tiles[4]).astype(bf16)
+    for n in range(6):
+        queries_ref[n] = (queries[n] * factor).astype(bf16)
+    new_keys_ref[...] = jnp.where(low, swap_half(turn[1]), swap_half(turn[4])).astype(bf16)
+    new_values_ref[...] = jnp.where(low, tiles[2], tiles[4]).astype(bf16)
+    lens_ref[...] = jnp.broadcast_to(lens, (128, LANES))
 
     loads[6].wait()
     loads[7].wait()
@@ -425,18 +431,40 @@
     own_bias = jnp.where(own, 0.0, FLOOR_SCORE).astype(f32)
     own_bias = jnp.concatenate([own_bias] * 6, axis=0)
     contract = (((1,), (1,)), ((), ()))
-    for block in range(4):
-        at = slice(32 * block, 32 * block + 32)
-        slots = slice(256 * block, 256 * block + 256)
-        query = jnp.concatenate([q[at] for q in queries], axis=0)
-        last = lens[at] - 1.0
+    place, side = me // 2, lax.rem(me, 2)
+
+    def send_parts(shift):
+        sent = []
+        for turned_side in range(2):
+            if shift == 0 and turned_side == 0:
+                continue
+            peer = 2 * lax.rem(place + shift, 4) + lax.rem(side + turned_side, 2)
+            copy = pltpu.make_async_remote_copy(
+                src_ref=att_send.at[rows_of(peer), :],
+                dst_ref=att_recv.at[me],
+                send_sem=seq_send.at[0, 2 * shift + turned_side],
+                recv_sem=seq_recv.at[0, 2 * shift + turned_side],
+                device_id=(peer, tp),
+                device_id_type=MESH,
+            )
+            copy.start()
+            sent.append(copy)
+        return sent
+
+    copies = []
+    for block in (2, 1, 3, 0):
+        number = lax.rem(place + block, 4)
+        at = pl.ds(pl.multiple_of(32 * number, 32), 32)
+        slots = pl.ds(pl.multiple_of(256 * number, 256), 256)
+        query = queries_ref[:, at, :].reshape(192, LANES)
+        last = lens_ref[at, 0:1] - 1.0
         back = last - slot
         older = last - (back - window * jnp.floor((back + 0.5) * (1.0 / window)))
         seen = (slot <= last) & ((slot < SINK) | (older > last + offset - window))
         old_bias = jnp.where(seen & same, 0.0, FLOOR_SCORE).astype(f32)
         old_bias = jnp.concatenate([old_bias] * 6, axis=0)
         old = lax.dot_general(query, keys_ref[slots, :], contract, preferred_element_type=f32)
-        new = lax.dot_general(query, new_keys[at], contract, preferred_element_type=f32)
+        new = lax.dot_general(query, new_keys_ref[at, :], contract, preferred_element_type=f32)
         old = old + old_bias
         new = new + own_bias
         top = jnp.maximum(
@@ -447,7 +475,7 @@
         mass = jnp.sum(old, axis=-1, keepdims=True) + jnp.sum(new, axis=-1, keepdims=True)
         mixed = jnp.dot(
             old.astype(bf16), values_ref[slots, :], preferred_element_type=f32
-        ) + jnp.dot(new.astype(bf16), new_values[at], preferred_element_type=f32)
+        ) + jnp.dot(new.astype(bf16), new_values_ref[at, :], preferred_element_type=f32)
         mixed = mixed / mass
         level = top + jnp.log(mass)
         head = [mixed[32 * n : 32 * n + 32] for n in range(6)]
@@ -467,10 +495,10 @@
         )
         att_send[at, 384:512] = jnp.where(lane32 < 24, levels, 0.0).astype(bf16)
 
-    pl.semaphore_wait(barrier, SEQ + TP - 2)
-    copies = seq_copies(
-        0, lambda peer: att_send.at[rows_of(peer), :], lambda index: att_recv.at[index]
-    )
+        if block == 1:
+            pl.semaphore_wait(barrier, SEQ + TP - 2)
+            copies += send_parts(2) + send_parts(1)
+    copies += send_parts(3) + send_parts(0)
     att_recv[me] = att_send[rows_of(me), :]
 
     loads[8].wait()
@@ -516,17 +544,18 @@
     att_all[tp] = jnp.concatenate(parts, axis=-1).astype(bf16)
 
     copies = [
-        tp_copy(step, att_all.at[tp], att_all.at[tp], lax.rem(tp + step, TP))
-        for step in range(1, TP)
+        tp_copy(step, att_all.at[tp], att_all.at[tp], peer)
+        for step, peer in enumerate((core_peer, far_peer, lax.rem(core_peer + 2, TP)))
     ]
     loads[11].wait()
     width = out_w_ref.shape[1]
     residual = tokens_ref[rows_of(me), pl.ds(pl.multiple_of(tp * width, 128), width)].astype(f32)
-    for copy in copies:
-        copy.wait()
-    for n in range(TP):
+    for step, group in enumerate((tp, core_peer, far_peer, lax.rem(core_peer + 2, TP))):
+        if step > 0:
+            copies[step - 1].wait()
+        at = pl.ds(pl.multiple_of(group * width, 128), width)
         residual = residual + jnp.dot(
-            att_all[n], out_w_ref[width * n : width * (n + 1), :], preferred_element_type=f32
+            att_all[group], out_w_ref[at, :], preferred_element_type=f32
         )
     res_own[...] = residual
     res_all[me] = residual.astype(bf16)
@@ -581,7 +610,8 @@
     groups = 4 // CHUNKS
     count = groups * TILE
     near, far, back = [], [], []
-    for chunk in range(CHUNKS):
+
+    def pick_theirs(chunk):
         first = 4 * (1 - core) + groups * chunk
         for n in range(groups):
             pick(first + n, 0)
@@ -589,13 +619,12 @@
         near.append(
             tp_copy(4 + chunk, picks.at[pl.ds(first, groups)], picks_recv.at[at], core_peer)
         )
-    for n in range(4):
-        pick(4 * core + n, 0)
-    sums_copy.wait()
-    ours = pl.ds(pl.multiple_of(64 * core, 64), 64)
-    sums_half[...] = split_pair(join_pair(sums[ours, :]) + join_pair(sums_recv[...]))
-    sums_copy = tp_copy(5 + 3 * CHUNKS, sums_half, sums_far, far_peer)
-    for chunk in range(CHUNKS):
+
+    def pick_ours(chunk):
+        for n in range(groups):
+            pick(4 * core + groups * chunk + n, 0)
+
+    def add_near(chunk):
         at = slice(groups * chunk, groups * (chunk + 1))
         mine = pl.ds(4 * core + groups * chunk, groups)
         near[chunk].wait()
@@ -603,6 +632,18 @@
         far.append(
             tp_copy(4 + CHUNKS + chunk, picks_half.at[at], picks_far.at[at], far_peer)
         )
+
+    ours = pl.ds(pl.multiple_of(64 * core, 64), 64)
+    pick_theirs(0)
+    pick_ours(0)
+    for chunk in range(1, CHUNKS):
+        pick_theirs(chunk)
+        add_near(chunk - 1)
+        pick_ours(chunk)
+    sums_copy.wait()
+    sums_half[...] = split_pair(join_pair(sums[ours, :]) + join_pair(sums_recv[...]))
+    sums_copy = tp_copy(5 + 3 * CHUNKS, sums_half, sums_far, far_peer)
+    add_near(CHUNKS - 1)
 
     sums_copy.wait()
     rows = join_pair(sums_half[...]) + join_pair(sums_far[...])
@@ -739,6 +780,10 @@
             pltpu.VMEM((64, LANES), bf16),
             pltpu.VMEM((64, LANES), bf16),
             pltpu.VMEM((TOP + 1, 64, LANES), f32),
+            pltpu.VMEM((6, count, LANES), bf16),
+            pltpu.VMEM((count, LANES), bf16),
+            pltpu.VMEM((count, LANES), bf16),
+            pltpu.VMEM((count, LANES), f32),
             pltpu.VMEM((8, TOP * TILE, LANES), bf16),
             pltpu.VMEM((count, EXPERTS * hidden), bf16),
             pltpu.VMEM((count, width), f32),

time: 39.9 us -> 39.4 us (0.987)
  Pallas kernels: 39.1 us -> 38.6 us
    pallas_call x1, Pallas kernels: 39.1 us -> 38.6 us  [fused_device(): pl.pallas_call(layer_kernel, out_shape=pltpu.VMEM((count, width), bf16),...]
where the time goes in v5:
time: 39.4 us; the launch traced here: 39.3 us
  Pallas kernels  38.6 us (98%)
  local copies, waits for them, and re-layouts  0.64 us (2%)
    pallas_call x1, Pallas kernels, fused_device(): pl.pallas_call(layer_kernel, out_shape=pltpu.VMEM((count, width), bf16),...  38.6 us

profile of v5, /device:TPU:0, one launch (start us, length us, event | category | flops | bytes accessed | tf_op | source)
XLA Modules:
  0.0 39.3 jit_solution(15598313514797477487)
XLA Ops:
  0.0 38.6 %layer.1 = bf16[128,384]{1,0:T(8,128)(2,1)S(1)} custom-call(bf16[128,1536]{1,0:T(8,128)(2,1)} %tokens_hbm.1, f32[1536]{0:T(1024)} %attn_gain_hbm.1, f32[384]{0:T(512)} %moe_gain_hbm.1, s32[1,32]{1,0:T(1,128)} %bitcast.13, s32[8,128]{1,0:T(8,128)} %bitcast.12, bf16[40,384]{1,0:T(8,128)(2,1)} %bitcast.11, bf16[1536,640]{1,0:T(8,128)(2,1)} %qkv_hbm.1, ...), custom_call_target="tpu_custom_call" | custom-call | flops 2000000000 | bytes 20000000 | tf_op jit(solution)/shard_map/layer/pallas_call | solution.py:746
  38.6 0.6 %copy.15 = bf16[128,384]{1,0:T(8,128)(2,1)} copy(bf16[128,384]{1,0:T(8,128)(2,1)S(1)} %layer.1) | data formatting | bytes 196608

commit v6 on v5

--- a/solution.py
+++ b/solution.py
@@ -183,7 +183,7 @@
 SEQ = 8
 TP = 4
 MESH = pl.DeviceIdType.MESH
-CHUNKS = 2
+CHUNKS = 4
 VMEM_LIMIT = 61 * 1024 * 1024
 TURN = 6.28125
 TURN_MIDDLE = 0.0019350051879882812
@@ -331,7 +331,7 @@
 
     def seq_copies(phase, source, target):
         copies = []
-        for step in range(1, SEQ):
+        for step in (4, 3, 5, 2, 6, 7, 1):
             peer = lax.rem(me + step, SEQ)
             copies.append(
                 pltpu.make_async_remote_copy(

time: 39.4 us -> 41.1 us (1.043)
  Pallas kernels: 38.6 us -> 40.4 us
    pallas_call x1, Pallas kernels: 38.6 us -> 40.4 us  [fused_device(): pl.pallas_call(layer_kernel, out_shape=pltpu.VMEM((count, width), bf16),...]
where the time goes in v6:
time: 41.1 us; the launch traced here: 41 us
  Pallas kernels  40.4 us (98%)
  local copies, waits for them, and re-layouts  0.64 us (2%)
    pallas_call x1, Pallas kernels, fused_device(): pl.pallas_call(layer_kernel, out_shape=pltpu.VMEM((count, width), bf16),...  40.4 us

profile of v6, /device:TPU:0, one launch (start us, length us, event | category | flops | bytes accessed | tf_op | source)
XLA Modules:
  0.0 41.0 jit_solution(13998664563176803564)
XLA Ops:
  0.0 40.4 %layer.1 = bf16[128,384]{1,0:T(8,128)(2,1)S(1)} custom-call(bf16[128,1536]{1,0:T(8,128)(2,1)} %tokens_hbm.1, f32[1536]{0:T(1024)} %attn_gain_hbm.1, f32[384]{0:T(512)} %moe_gain_hbm.1, s32[1,32]{1,0:T(1,128)} %bitcast.13, s32[8,128]{1,0:T(8,128)} %bitcast.12, bf16[40,384]{1,0:T(8,128)(2,1)} %bitcast.11, bf16[1536,640]{1,0:T(8,128)(2,1)} %qkv_hbm.1, ...), custom_call_target="tpu_custom_call" | custom-call | flops 2000000000 | bytes 20000000 | tf_op jit(solution)/shard_map/layer/pallas_call | solution.py:746
  40.4 0.6 %copy.15 = bf16[128,384]{1,0:T(8,128)(2,1)} copy(bf16[128,384]{1,0:T(8,128)(2,1)S(1)} %layer.1) | data formatting | bytes 196608

commit v7 on v5

--- a/solution.py
+++ b/solution.py
@@ -258,6 +258,7 @@
     res_own,
     res_all,
     pair_w,
+    turned_w,
     dense,
     onehot,
     shifted,
@@ -517,6 +518,14 @@
         return carry
 
     lax.fori_loop(0, 8, mark, 0, unroll=2)
+    loads[12].wait()
+    loads[13].wait()
+
+    def turn_pair(n, carry):
+        turned_w[n] = jnp.transpose(pair_w[pl.ds(2 * n, 2)].reshape(2 * LANES, -1))
+        return carry
+
+    lax.fori_loop(0, EXPERTS // 4, turn_pair, 0, unroll=2)
     half_lane = jnp.where(low, 0, 1)
     for k in range(TOP):
         shifted[k] = routes_ref[:, k : k + 1] - half_lane
@@ -560,6 +569,7 @@
     res_own[...] = residual
     res_all[me] = residual.astype(bf16)
     copies = seq_copies(1, lambda peer: res_all.at[me], lambda index: res_all.at[index])
+    lax.fori_loop(EXPERTS // 4, EXPERTS // 2, turn_pair, 0, unroll=2)
     for copy in copies:
         copy.wait()
 
@@ -586,14 +596,8 @@
         core_peer,
     )
 
-    loads[12].wait()
-    loads[13].wait()
-
     def experts(n, carry):
-        weight = pair_w[pl.ds(2 * n, 2)].reshape(2 * LANES, width)
-        both = lax.dot_general(
-            gained_b, weight, contract, preferred_element_type=f32
-        ).astype(bf16)
+        both = jnp.dot(gained_b, turned_w[n], preferred_element_type=f32).astype(bf16)
         dense[2 * n] = both[:, :LANES]
         dense[2 * n + 1] = both[:, LANES:]
         return carry
@@ -767,6 +771,7 @@
             pltpu.VMEM((TILE, width), f32),
             pltpu.VMEM((SEQ, TILE, width), bf16),
             pltpu.VMEM((EXPERTS, 2 * hidden, width), bf16),
+            pltpu.VMEM((EXPERTS // 2, width, 4 * hidden), bf16),
             pltpu.VMEM((EXPERTS, count, LANES), bf16),
             pltpu.VMEM((8, TOP * TILE, EXPERTS * TILE), bf16),
             pltpu.VMEM((TOP, count, LANES), jnp.int32),

time: 39.4 us -> 38.9 us (0.987)
  Pallas kernels: 38.6 us -> 38.1 us
    pallas_call x1, Pallas kernels: 38.6 us -> 38.1 us  [fused_device(): pl.pallas_call(layer_kernel, out_shape=pltpu.VMEM((count, width), bf16),...]
where the time goes in v7:
time: 38.9 us; the launch traced here: 38.8 us
  Pallas kernels  38.1 us (98%)
  local copies, waits for them, and re-layouts  0.64 us (2%)
    pallas_call x1, Pallas kernels, fused_device(): pl.pallas_call(layer_kernel, out_shape=pltpu.VMEM((count, width), bf16),...  38.1 us

profile of v7, /device:TPU:0, one launch (start us, length us, event | category | flops | bytes accessed | tf_op | source)
XLA Modules:
  0.0 38.8 jit_solution(16164122891479658745)
XLA Ops:
  0.0 38.1 %layer.1 = bf16[128,384]{1,0:T(8,128)(2,1)S(1)} custom-call(bf16[128,1536]{1,0:T(8,128)(2,1)} %tokens_hbm.1, f32[1536]{0:T(1024)} %attn_gain_hbm.1, f32[384]{0:T(512)} %moe_gain_hbm.1, s32[1,32]{1,0:T(1,128)} %bitcast.13, s32[8,128]{1,0:T(8,128)} %bitcast.12, bf16[40,384]{1,0:T(8,128)(2,1)} %bitcast.11, bf16[1536,640]{1,0:T(8,128)(2,1)} %qkv_hbm.1, ...), custom_call_target="tpu_custom_call" | custom-call | flops 2000000000 | bytes 20000000 | tf_op jit(solution)/shard_map/layer/pallas_call | solution.py:750
  38.1 0.6 %copy.15 = bf16[128,384]{1,0:T(8,128)(2,1)} copy(bf16[128,384]{1,0:T(8,128)(2,1)S(1)} %layer.1) | data formatting | bytes 196608
